TPU v7x, 32 devices: a whole 2x2x4 slice. The times are simulated.
32 devices in a mesh: section: 2 (over y), wide: 4 (over z), narrow: 4 (over x, core).
Axes of the slice: x: 2, y: 2, z: 4, core: 2. Of those that a mesh axis runs over, the one named last changes fastest.
Arguments:
- saved_inputs: bfloat16 [2, 512, 8192], P('section', None, 'narrow'), may hold values from -6 to 6
- upstream: bfloat16 [512, 8192], P('wide', 'narrow'), may hold values from -6 to 6
- up_weight: bfloat16 [2, 8192, 16384], P('section', 'narrow', 'wide'), may hold values from -0.0625 to 0.0625
- down_weight: bfloat16 [2, 16384, 8192], P('section', 'wide', 'narrow'), may hold values from -0.046875 to 0.046875
Outputs:
- boundary_grads: bfloat16 [2, 512, 8192], P('section', 'wide', 'narrow')
- up_grads: bfloat16 [2, 8192, 16384], P('section', 'narrow', 'wide')
- down_grads: bfloat16 [2, 16384, 8192], P('section', 'wide', 'narrow')
All inputs are finite; a program needn't handle non-finite values.
Results may differ from a plain program's by a relative error of at most 0.028.
Values may be sent and summed in bfloat16 or wider, within the bound.
A program may use at most 192 MiB of HBM per device.

v0:
```python
import jax
import jax.numpy as jnp
from jax import lax
from jax.sharding import PartitionSpec as P

gelu_scale = 0.7978845608028654
cubic_term = 0.044715


def from_behind(block, axis, distance):
    devices = range(lax.axis_size(axis))
    route = [(i - distance, i) for i in devices if i - distance in devices]
    return lax.ppermute(block, axis, route)


def gelu_parts(pre_act):
    inner = jnp.tanh(gelu_scale * (pre_act + cubic_term * pre_act * pre_act * pre_act))
    act_value = 0.5 * pre_act * (1.0 + inner)
    slopes = 0.5 * (1.0 + inner) + 0.5 * pre_act * (1.0 - inner * inner) * gelu_scale * (
        1.0 + 3.0 * cubic_term * pre_act * pre_act
    )
    return (act_value, slopes)


def contract_rows(first_op, second_op):
    return lax.dot_general(
        first_op, second_op, (((0,), (0,)), ((), ())), preferred_element_type=jnp.float32
    )


def contract_cols(first_op, second_op):
    return lax.dot_general(
        first_op, second_op, (((1,), (1,)), ((), ())), preferred_element_type=jnp.float32
    )


def layer_back(whole_grad, saved_rows, w_up, w_down):
    tokens_all = whole_grad.shape[0]
    rows_wide = tokens_all // lax.axis_size("wide")
    picked = saved_rows
    pre_share = lax.psum_scatter(
        jnp.dot(picked, w_up, preferred_element_type=jnp.float32).astype(jnp.bfloat16),
        "narrow",
        scatter_dimension=0,
        tiled=True,
    ).astype(jnp.float32)
    act_share, slope_share = gelu_parts(pre_share)
    hidden = lax.all_gather(act_share.astype(jnp.bfloat16), "narrow", axis=0, tiled=True)
    grad_down = contract_rows(hidden, whole_grad).astype(jnp.bfloat16)
    picked = whole_grad
    back_share = lax.psum_scatter(
        contract_cols(picked, w_down).astype(jnp.bfloat16),
        "narrow",
        scatter_dimension=0,
        tiled=True,
    ).astype(jnp.float32)
    slope_part = (back_share * slope_share).astype(jnp.bfloat16)
    slope_grad = lax.all_gather(slope_part, "narrow", axis=0, tiled=True)
    grad_up = contract_rows(saved_rows, slope_grad).astype(jnp.bfloat16)
    picked = slope_grad
    summed = lax.psum_scatter(
        contract_cols(picked, w_up).astype(jnp.bfloat16), "wide", scatter_dimension=0, tiled=True
    ).astype(jnp.float32)
    own_rows = lax.dynamic_slice_in_dim(
        whole_grad, lax.axis_index("wide") * rows_wide, rows_wide, 0
    )
    grad_in = (own_rows.astype(jnp.float32) + summed).astype(jnp.bfloat16)
    return (grad_in, grad_up, grad_down)


def body(saved_inputs, upstream, up_weight, down_weight):
    saved_rows = saved_inputs[0]
    w_up = up_weight[0]
    w_down = down_weight[0]
    first_whole = lax.all_gather(upstream, "wide", axis=0, tiled=True)
    upper_in, upper_up, upper_down = layer_back(first_whole, saved_rows, w_up, w_down)
    assembled = lax.all_gather(upper_in, "wide", axis=0, tiled=True)
    second_whole = from_behind(assembled, "section", -1)
    lower_in, lower_up, lower_down = layer_back(second_whole, saved_rows, w_up, w_down)
    is_upper = lax.axis_index("section") == 1

    def pick_section(upper_part, lower_part):
        return jnp.where(is_upper, upper_part, lower_part)[None]

    return (
        pick_section(upper_in, lower_in),
        pick_section(upper_up, lower_up),
        pick_section(upper_down, lower_down),
    )


def solution(mesh):
    placed = (
        P("section", None, "narrow"),
        P("wide", "narrow"),
        P("section", "narrow", "wide"),
        P("section", "wide", "narrow"),
    )
    return jax.shard_map(
        body,
        mesh=mesh,
        in_specs=placed,
        out_specs=(
            P("section", "wide", "narrow"),
            P("section", "narrow", "wide"),
            P("section", "wide", "narrow"),
        ),
        check_vma=False,
    )
```

profile of v0, /device:TPU:0, one launch (start us, length us, event | category | flops | bytes accessed | tf_op | source)
XLA Modules:
  0.0 515.7 jit_solution(12745934264674531991)
XLA Ops:
  9.6 13.7 %fusion.10 = bf16[512,4096]{1,0:T(8,128)(2,1)} fusion(bf16[1,2048,4096]{2,1,0:T(8,128)(2,1)} %param.6, bf16[1,512,2048]{2,1,0:T(8,128)(2,1)S(1)} %copy-done), kind=kOutput, calls=%fused_computation.12 | convolution fusion | flops 8592031744 | bytes 23068672 | tf_op jit(solution)/shard_map/dot_general | solution.py:42
  23.4 35.7 %all-gather.6.cloned.1.call-done = bf16[512,2048]{1,0:T(8,128)(2,1)} async-done(((bf16[128,2048]{1,0:T(8,128)(2,1)}), bf16[512,2048]{1,0:T(8,128)(2,1)}) %all-gather.6.cloned.1.call-update) | async-done | bytes 2097168 | tf_op jit(solution)/shard_map/all_gather | solution.py:75
  59.1 14.4 %fusion.13 = bf16[512,4096]{1,0:T(8,128)(2,1)} fusion(bf16[512,2048]{1,0:T(8,128)(2,1)} %all-gather.6.cloned.1.call-done, bf16[1,4096,2048]{2,1,0:T(8,128)(2,1)} %param.7), kind=kOutput, calls=%fused_computation.13 | convolution fusion | flops 8592031744 | bytes 23068672 | tf_op jit(solution)/shard_map/dot_general | solution.py:32
  73.6 44.6 %reduce-scatter.6.cloned.1.call-done = bf16[128,4096]{1,0:T(8,128)(2,1)} async-done(((bf16[512,4096]{1,0:T(8,128)(2,1)}), bf16[128,4096]{1,0:T(8,128)(2,1)}) %reduce-scatter.6.cloned.1.call-update) | async-done | bytes 1048592 | tf_op jit(solution)/shard_map/reduce_scatter | solution.py:51
  118.2 4.0 multiply_convert_fusion.1
  122.4 34.2 %all-gather.8.cloned.1.call-done = bf16[512,4096]{1,0:T(8,128)(2,1)} async-done(((bf16[128,4096]{1,0:T(8,128)(2,1)}), bf16[512,4096]{1,0:T(8,128)(2,1)}) %all-gather.8.cloned.1.call-update) | async-done | bytes 4194320 | tf_op jit(solution)/shard_map/all_gather | solution.py:58
  156.6 14.6 %fusion.19 = bf16[512,2048]{1,0:T(8,128)(2,1)} fusion(bf16[512,4096]{1,0:T(8,128)(2,1)} %all-gather.8.cloned.1.call-done, bf16[1,2048,4096]{2,1,0:T(8,128)(2,1)} %param.6), kind=kOutput, calls=%fused_computation.22 | convolution fusion | flops 8590983168 | bytes 23068672 | tf_op jit(solution)/shard_map/dot_general | solution.py:32
  171.3 44.0 %reduce-scatter.10.cloned.1.call-done = bf16[128,2048]{1,0:T(8,128)(2,1)} async-done(((bf16[512,2048]{1,0:T(8,128)(2,1)}), bf16[128,2048]{1,0:T(8,128)(2,1)}) %reduce-scatter.10.cloned.1.call-update) | async-done | bytes 524304 | tf_op jit(solution)/shard_map/reduce_scatter | solution.py:61
  215.3 2.1 add_convert_fusion.1
  217.5 45.3 %all-gather.10.cloned.1.call-done = bf16[512,2048]{1,0:T(8,128)(2,1)} async-done(((bf16[128,2048]{1,0:T(8,128)(2,1)}), bf16[512,2048]{1,0:T(8,128)(2,1)}) %all-gather.10.cloned.1.call-update) | async-done | bytes 2097168 | tf_op jit(solution)/shard_map/all_gather | solution.py:77
  264.1 48.2 %collective-permute-done = bf16[512,2048]{1,0:T(8,128)(2,1)S(1)} collective-permute-done((bf16[512,2048]{1,0:T(8,128)(2,1)}, bf16[512,2048]{1,0:T(8,128)(2,1)S(1)}, u32[]{:S(2)}, u32[]{:S(2)}) %collective-permute-start) | collective-permute-done | bytes 2097184 | tf_op jit(solution)/shard_map/ppermute | solution.py:13
  313.6 13.8 %fusion.16 = bf16[512,4096]{1,0:T(8,128)(2,1)} fusion(bf16[512,2048]{1,0:T(8,128)(2,1)S(1)} %collective-permute-done, bf16[1,4096,2048]{2,1,0:T(8,128)(2,1)} %param.7), kind=kOutput, calls=%fused_computation.14 | convolution fusion | flops 8592031744 | bytes 23068672 | tf_op jit(solution)/shard_map/dot_general | solution.py:32
  327.5 42.5 %reduce-scatter.12.cloned.1.call-done = bf16[128,4096]{1,0:T(8,128)(2,1)} async-done(((bf16[512,4096]{1,0:T(8,128)(2,1)}), bf16[128,4096]{1,0:T(8,128)(2,1)}) %reduce-scatter.12.cloned.1.call-update) | async-done | bytes 1048592 | tf_op jit(solution)/shard_map/reduce_scatter | solution.py:51
  370.0 4.1 fusion.30
  375.1 14.8 %fusion.35 = bf16[4096,2048]{1,0:T(8,128)(2,1)} fusion(bf16[512,4096]{1,0:T(8,128)(2,1)} %all-gather.8.cloned.1.call-done, bf16[1,512,2048]{2,1,0:T(8,128)(2,1)S(1)} %copy-done), kind=kOutput, calls=%fused_computation.34 | convolution fusion | flops 8589934592 | bytes 23068672 | tf_op jit(solution)/shard_map/dot_general | solution.py:26
  389.8 18.7 %all-gather.12.cloned.1.call-done = bf16[512,4096]{1,0:T(8,128)(2,1)} async-done(((bf16[128,4096]{1,0:T(8,128)(2,1)}), bf16[512,4096]{1,0:T(8,128)(2,1)}) %all-gather.12.cloned.1.call-update) | async-done | bytes 4194320 | tf_op jit(solution)/shard_map/all_gather | solution.py:58
  408.5 14.8 %select_bitcast_fusion.1 = bf16[1,2048,4096]{1,2,0:T(8,128)(2,1)} fusion(bf16[4096,2048]{1,0:T(8,128)(2,1)} %fusion.35, pred[]{:T(512)S(6)} %eq.3, bf16[512,4096]{1,0:T(8,128)(2,1)} %all-gather.12.cloned.1.call-done, bf16[1,512,2048]{2,1,0:T(8,128)(2,1)S(1)} %copy-done), kind=kOutput, calls=%fused_computation.11 | convolution fusion | flops 8606711808 | bytes 39845888 | tf_op jit(solution)/shard_map/dot_general | solution.py:26
  423.3 21.2 %copy.7 = bf16[1,2048,4096]{2,1,0:T(8,128)(2,1)} copy(bf16[1,2048,4096]{1,2,0:T(8,128)(2,1)} %select_bitcast_fusion.1) | data formatting | bytes 33554432
  444.6 14.9 %fusion.22 = bf16[512,2048]{1,0:T(8,128)(2,1)} fusion(bf16[512,4096]{1,0:T(8,128)(2,1)} %all-gather.12.cloned.1.call-done, bf16[1,2048,4096]{2,1,0:T(8,128)(2,1)} %param.6), kind=kOutput, calls=%fused_computation.23 | convolution fusion | flops 8590983168 | bytes 23068672 | tf_op jit(solution)/shard_map/dot_general | solution.py:32
  459.5 1.5 copy-done.4
  461.0 14.7 %fusion.40 = bf16[4096,2048]{1,0:T(8,128)(2,1)} fusion(bf16[512,4096]{1,0:T(8,128)(2,1)} %all-gather.14.cloned.1.call-done, bf16[512,2048]{1,0:T(8,128)(2,1)S(1)} %copy-done.4), kind=kOutput, calls=%fused_computation.43 | convolution fusion | flops 8589934592 | bytes 23068672 | tf_op jit(solution)/shard_map/dot_general | solution.py:26
  475.7 15.6 %select_bitcast_fusion = bf16[1,4096,2048]{2,1,0:T(8,128)(2,1)} fusion(bf16[4096,2048]{1,0:T(8,128)(2,1)} %fusion.40, pred[]{:T(512)S(6)} %eq.3, bf16[512,4096]{1,0:T(8,128)(2,1)} %all-gather.14.cloned.1.call-done, bf16[512,2048]{1,0:T(8,128)(2,1)} %copy-done.5), kind=kOutput, calls=%fused_computation.10 | convolution fusion | flops 8606711808 | bytes 39845888 | tf_op jit(solution)/shard_map/dot_general | solution.py:26
  491.4 14.5 %reduce-scatter.14.cloned.1.call-done = bf16[128,2048]{1,0:T(8,128)(2,1)} async-done(((bf16[512,2048]{1,0:T(8,128)(2,1)}), bf16[128,2048]{1,0:T(8,128)(2,1)}) %reduce-scatter.14.cloned.1.call-update) | async-done | bytes 524304 | tf_op jit(solution)/shard_map/reduce_scatter | solution.py:61
  505.9 2.2 fusion.39
  (34 shorter events, 5.8 us)
Async XLA Ops:
  8.0 1.6 copy-start
  8.0 51.1 %all-gather.6.cloned.1.call-start = ((), (), s32[]{:S(2)}) async-start(), calls=%async_computation.5 | async-start | bytes 2621440 | tf_op jit(solution)/shard_map/all_gather | solution.py:75
  8.7 64.9 %reduce-scatter.8.cloned.1.call-start = ((), (), s32[]{:S(2)}) async-start(), calls=%async_computation.7 | async-start | bytes 5242880 | tf_op jit(solution)/shard_map/reduce_scatter | solution.py:41
  23.3 94.9 %reduce-scatter.6.cloned.1.call-start = ((), (), s32[]{:S(2)}) async-start(), calls=%async_computation.6 | async-start | bytes 5242880 | tf_op jit(solution)/shard_map/reduce_scatter | solution.py:51
  73.5 83.1 %all-gather.8.cloned.1.call-start = ((), (), s32[]{:S(2)}) async-start(), calls=%async_computation.8 | async-start | bytes 5242880 | tf_op jit(solution)/shard_map/all_gather | solution.py:58
  122.2 93.1 %reduce-scatter.10.cloned.1.call-start = ((), (), s32[]{:S(2)}) async-start(), calls=%async_computation.9 | async-start | bytes 2621440 | tf_op jit(solution)/shard_map/reduce_scatter | solution.py:61
  171.2 91.6 %all-gather.10.cloned.1.call-start = ((), (), s32[]{:S(2)}) async-start(), calls=%async_computation.10 | async-start | bytes 2621440 | tf_op jit(solution)/shard_map/all_gather | solution.py:77
  217.4 152.5 %reduce-scatter.12.cloned.1.call-start = ((), (), s32[]{:S(2)}) async-start(), calls=%async_computation.11 | async-start | bytes 5242880 | tf_op jit(solution)/shard_map/reduce_scatter | solution.py:51
  262.8 49.5 %collective-permute-start = (bf16[512,2048]{1,0:T(8,128)(2,1)}, bf16[512,2048]{1,0:T(8,128)(2,1)S(1)}, u32[]{:S(2)}, u32[]{:S(2)}) collective-permute-start(bf16[512,2048]{1,0:T(8,128)(2,1)} %all-gather.10.cloned.1.call-done), channel_id=1, source_target_pairs={{16,0},{17,1},{18,2},{19,3},{20,4},{21,5},{22,6},{23,7},{24,8},{25... | collective-permute-start | bytes 6291464 | tf_op jit(solution)/shard_map/ppermute | solution.py:13
  312.3 1.3 copy-start.5
  327.4 42.6 %copy-start.3 = (bf16[128,4096]{1,0:T(8,128)(2,1)S(1)}, bf16[128,4096]{1,0:T(8,128)(2,1)}, u32[]{:S(2)}) copy-start(bf16[128,4096]{1,0:T(8,128)(2,1)} %reduce-scatter.8.cloned.1.call-done) | copy-start | bytes 3145732
  327.4 81.1 %all-gather.12.cloned.1.call-start = ((), (), s32[]{:S(2)}) async-start(), calls=%async_computation.12 | async-start | bytes 5242880 | tf_op jit(solution)/shard_map/all_gather | solution.py:58
  374.1 85.4 %all-gather.14.cloned.1.call-start = ((), (), s32[]{:S(2)}) async-start(), calls=%async_computation.14 | async-start | bytes 5242880 | tf_op jit(solution)/shard_map/all_gather | solution.py:48
  374.8 131.0 %reduce-scatter.14.cloned.1.call-start = ((), (), s32[]{:S(2)}) async-start(), calls=%async_computation.13 | async-start | bytes 2621440 | tf_op jit(solution)/shard_map/reduce_scatter | solution.py:61
  459.4 1.6 copy-start.4
  475.7 30.1 %copy-start.2 = (bf16[128,2048]{1,0:T(8,128)(2,1)S(1)}, bf16[128,2048]{1,0:T(8,128)(2,1)}, u32[]{:S(2)}) copy-start(bf16[128,2048]{1,0:T(8,128)(2,1)} %add_convert_fusion.1) | copy-start | bytes 1572868
  475.7 32.3 %copy-start.1 = (bf16[1,512,2048]{2,1,0:T(8,128)(2,1)S(1)}, bf16[1,512,2048]{2,1,0:T(8,128)(2,1)}, u32[]{:S(2)}) copy-start(bf16[1,512,2048]{2,1,0:T(8,128)(2,1)} %param.4) | copy-start | bytes 6291460
Sparse Core Ops, SparseCore 0:
  10.4 48.6 all-gather.5
  171.4 43.8 reduce-scatter.9
  217.5 45.2 all-gather.9
  459.6 46.2 reduce-scatter.13
Sparse Core Ops, SparseCore 1:
  23.4 47.1 reduce-scatter.7
  73.7 44.4 reduce-scatter.5
  122.3 34.3 all-gather.7
  327.5 42.4 reduce-scatter.11
  374.2 34.3 all-gather.11
  410.2 34.3 all-gather.13
where the time goes:
time: 523 us; the launch traced here: 516 us
  waiting for transfers between devices  329 us (63%)
  matrix products  131 us (25%)
  local copies, waits for them, and re-layouts  24.9 us (5%)
  between operations  15.8 us (3%)
  other arithmetic  12.4 us (2%)
    reduce_scatter x2, waiting for transfers between devices, layer_back(): lax.psum_scatter(contract_cols(picked, w_down).astype(jnp.bfloat16), 'nar...  87.1 us
    dot_general x4, matrix products, contract_rows(): lax.dot_general(first_op, second_op, (((0,), (0,)), ((), ())), preferred_...  59.9 us
    reduce_scatter x2, waiting for transfers between devices, layer_back(): lax.psum_scatter(contract_cols(picked, w_up).astype(jnp.bfloat16), 'wide'...  58.5 us
    dot_general x4, matrix products, contract_cols(): lax.dot_general(first_op, second_op, (((1,), (1,)), ((), ())), preferred_...  57.7 us
    all_gather x2, waiting for transfers between devices, layer_back(): slope_grad = lax.all_gather(slope_part, 'narrow', axis=0, tiled=True)  52.9 us
    ppermute x1, waiting for transfers between devices, from_behind(): return lax.ppermute(block, axis, route)  48.2 us
    all_gather x1, waiting for transfers between devices, body(): assembled = lax.all_gather(upper_in, 'wide', axis=0, tiled=True)  45.3 us
    all_gather x1, waiting for transfers between devices, body(): first_whole = lax.all_gather(upstream, 'wide', axis=0, tiled=True)  35.7 us
  transfers between devices with their start and end apart: 11, of which 9 were waited for; matrix products, arithmetic and copies ran while one was open for 24% of the time, Pallas kernels for 0%

commit v1 on v0

v1 whole, which is shorter than its diff:
```python
import jax
import jax.numpy as jnp
from jax import lax
from jax.sharding import PartitionSpec as P

gelu_scale = 0.7978845608028654
cubic_term = 0.044715
CHUNK_ROWS = 32


def shifted(block, axis, distance):
    size = lax.axis_size(axis)
    return lax.ppermute(block, axis, [(i, (i + distance) % size) for i in range(size)])


def from_partner(block):
    size = lax.axis_size("narrow")
    return lax.ppermute(block, "narrow", [(i, i ^ 1) for i in range(size)])


def gelu_parts(pre_act):
    inner = jnp.tanh(gelu_scale * (pre_act + cubic_term * pre_act * pre_act * pre_act))
    act_value = 0.5 * pre_act * (1.0 + inner)
    slopes = 0.5 * (1.0 + inner) + 0.5 * pre_act * (1.0 - inner * inner) * gelu_scale * (
        1.0 + 3.0 * cubic_term * pre_act * pre_act
    )
    return (act_value, slopes)


def contract_rows(first_op, second_op):
    return lax.dot_general(
        first_op, second_op, (((0,), (0,)), ((), ())), preferred_element_type=jnp.float32
    )


def contract_cols(first_op, second_op):
    return lax.dot_general(
        first_op, second_op, (((1,), (1,)), ((), ())), preferred_element_type=jnp.float32
    )


def sum_half(part, is_odd):
    half = part.shape[1] // 2
    low, high = part[:, :half], part[:, half:]
    got = from_partner(jnp.where(is_odd, low, high))
    mine = jnp.where(is_odd, high, low)
    chip = (mine.astype(jnp.float32) + got.astype(jnp.float32)).astype(jnp.bfloat16)
    total = chip.astype(jnp.float32)
    for step in range(1, lax.axis_size("narrow") // 2):
        total = total + shifted(chip, "narrow", 2 * step).astype(jnp.float32)
    return total


def both_halves(mine, is_odd):
    other = from_partner(mine)
    return jnp.concatenate(
        [jnp.where(is_odd, other, mine), jnp.where(is_odd, mine, other)], axis=1
    )


def gather_wide(rows):
    wide = lax.axis_size("wide")
    return jnp.concatenate([rows] + [shifted(rows, "wide", j) for j in range(1, wide)], axis=0)


def scatter_wide(part, own_rows):
    wide = lax.axis_size("wide")
    rows = part.shape[0] // wide
    total = own_rows.astype(jnp.float32) + part[:rows].astype(jnp.float32)
    for j in range(1, wide):
        block = part[j * rows : (j + 1) * rows]
        total = total + shifted(block, "wide", -j).astype(jnp.float32)
    return total.astype(jnp.bfloat16)


def body(saved_inputs, upstream, up_weight, down_weight):
    w_up = up_weight[0]
    w_down = down_weight[0]
    wide = lax.axis_size("wide")
    place = lax.axis_index("wide")
    is_odd = lax.axis_index("narrow") % 2 == 1
    is_upper = lax.axis_index("section") == 1
    tokens, width = saved_inputs.shape[1:]
    rows = min(CHUNK_ROWS, tokens // wide)
    chunks = tokens // wide // rows

    blocks = saved_inputs[0].reshape(wide, chunks, rows, width)
    blocks = [
        lax.dynamic_index_in_dim(blocks, lax.rem(place + wide - j, wide), 0, keepdims=False)
        for j in range(wide)
    ]
    saved = [
        jnp.concatenate([block[c] for block in blocks], axis=0) for c in range(chunks)
    ]
    own = [upstream[c * rows : (c + 1) * rows] for c in range(chunks)]

    def backward(incoming, own_rows, slopes):
        back = sum_half(contract_cols(incoming, w_down).astype(jnp.bfloat16), is_odd)
        slope = both_halves((back * slopes).astype(jnp.bfloat16), is_odd)
        part = contract_cols(slope, w_up).astype(jnp.bfloat16)
        return slope, scatter_wide(part, own_rows)

    hidden, slopes, second = [], [], []
    for c in range(chunks):
        first_in = gather_wide(own[c])
        part = jnp.dot(saved[c], w_up, preferred_element_type=jnp.float32).astype(jnp.bfloat16)
        act, slope_of = gelu_parts(sum_half(part, is_odd))
        hidden.append(both_halves(act.astype(jnp.bfloat16), is_odd))
        slopes.append(slope_of)
        _, grad = backward(first_in, own[c], slope_of)
        second.append(lax.ppermute(grad, "section", [(1, 0)]))
    incoming, slope, grads = [], [], []
    for c in range(chunks):
        own_rows = jnp.where(is_upper, own[c], second[c])
        incoming.append(gather_wide(own_rows))
        one_slope, grad = backward(incoming[c], own_rows, slopes[c])
        slope.append(one_slope)
        grads.append(grad)
    grad_down = contract_rows(
        jnp.concatenate(hidden, axis=0), jnp.concatenate(incoming, axis=0)
    ).astype(jnp.bfloat16)
    grad_up = contract_rows(
        jnp.concatenate(saved, axis=0), jnp.concatenate(slope, axis=0)
    ).astype(jnp.bfloat16)
    return jnp.concatenate(grads, axis=0)[None], grad_up[None], grad_down[None]


def solution(mesh):
    placed = (
        P("section", None, "narrow"),
        P("wide", "narrow"),
        P("section", "narrow", "wide"),
        P("section", "wide", "narrow"),
    )
    return jax.shard_map(
        body,
        mesh=mesh,
        in_specs=placed,
        out_specs=(
            P("section", "wide", "narrow"),
            P("section", "narrow", "wide"),
            P("section", "wide", "narrow"),
        ),
        check_vma=False,
    )
```

time: 523 us -> 582 us (1.11)
  waiting for transfers between devices: 329 us -> 141 us
  matrix products: 131 us -> 248 us
  starting transfers between devices: 2.09 us -> 93 us
  other arithmetic: 12.4 us -> 60.4 us
  between operations: 15.8 us -> 2.16 us
    reduce_scatter x5 -> x0, waiting for transfers between devices: 146 us -> none  [the longest x2 87.1 us: layer_back(): lax.psum_scatter(contract_cols(picked, w_down).astype(jnp.bfloat16), 'nar...]
    all_gather x5 -> x0, waiting for transfers between devices: 134 us -> none  [the longest x2 52.9 us: layer_back(): slope_grad = lax.all_gather(slope_part, 'narrow', axis=0, tiled=True)]
    dot_general x4 -> x16, matrix products: 57.7 us -> 188 us  [contract_cols(): lax.dot_general(first_op, second_op, (((1,), (1,)), ((), ())), preferred_...]
    ppermute x1 -> x88, waiting for transfers between devices: 48.2 us -> 141 us  [the longest x60 138 us: shifted(): lax.ppermute(block, axis, [(i, (i + distance) % size) for i in range(size)])]
    ppermute x1 -> x88, starting transfers between devices: 1.28 us -> 93 us  [the longest x60 83.3 us: shifted(): lax.ppermute(block, axis, [(i, (i + distance) % size) for i in range(size)])]
    select_n x0 -> x24, other arithmetic: none -> 26 us  [the longest x12 15.3 us: both_halves(): jnp.where(is_odd, other, mine)]
    convert_element_type x3 -> x26, other arithmetic: 10.2 us -> 29.1 us  [the longest x12 10.5 us: sum_half(): (mine.astype(jnp.float32) + got.astype(jnp.float32)).astype(jnp.bfloat16)]
    dot_general x4 -> x2, matrix products: 59.9 us -> 43.9 us  [contract_rows(): lax.dot_general(first_op, second_op, (((0,), (0,)), ((), ())), preferred_...]
  transfers between devices with their start and end apart: 11 -> 88, of which waited for: 9 -> 16; matrix products, arithmetic and copies ran while one was open for 24% -> 57% of each run, Pallas kernels for 0% -> 0%
where the time goes in v1:
time: 582 us; the launch traced here: 573 us
  matrix products  248 us (43%)
  waiting for transfers between devices  141 us (24%)
  starting transfers between devices  93 us (16%)
  other arithmetic  60.4 us (10%)
  local copies, waits for them, and re-layouts  28.5 us (5%)
    dot_general x16, matrix products, contract_cols(): lax.dot_general(first_op, second_op, (((1,), (1,)), ((), ())), preferred_...  188 us
    ppermute x60, waiting for transfers between devices, shifted(): lax.ppermute(block, axis, [(i, (i + distance) % size) for i in range(size)])  138 us
    ppermute x60, starting transfers between devices, shifted(): lax.ppermute(block, axis, [(i, (i + distance) % size) for i in range(size)])  83.3 us
    dot_general x2, matrix products, contract_rows(): lax.dot_general(first_op, second_op, (((0,), (0,)), ((), ())), preferred_...  43.9 us
    unnamed x128, local copies, waits for them, and re-layouts  18.2 us
    dot_general x4, matrix products, body(): jnp.dot(saved[c], w_up, preferred_element_type=jnp.float32)  16.4 us
    select_n x12, other arithmetic, both_halves(): jnp.where(is_odd, other, mine)  15.3 us
  transfers between devices with their start and end apart: 88, of which 16 were waited for; matrix products, arithmetic and copies ran while one was open for 57% of the time, Pallas kernels for 0%

profile of v1, /device:TPU:0, one launch (start us, length us, event | category | flops | bytes accessed | tf_op | source)
XLA Modules:
  0.0 573.2 jit_solution(4927905802958397628)
XLA Ops:
  15.3 9.1 %fusion.73 = bf16[128,4096]{1,0:T(8,128)(2,1)S(1)} fusion(bf16[1,2048,4096]{2,1,0:T(8,128)(2,1)} %param.6, bf16[32,2048]{1,0:T(8,128)(2,1)S(1)} %get-tuple-element.12, bf16[32,2048]{1,0:T(8,128)(2,1)S(1)} %get-tuple-element.14, bf16[32,2048]{1,0:T(8,128)(2,1)S(1)} %get-tuple-element.16, bf16[32,2048]{1,0:T(8,128)(2,1)S(1)} %get-tuple-element.18), kind=kOutput, calls=%fused_computation.53 | convolution fusion | flops 2150105088 | bytes 18350080 | tf_op jit(solution)/shard_map/dot_general | solution.py:106
  42.4 11.4 %fusion.52 = bf16[128,4096]{1,0:T(8,128)(2,1)S(1)} fusion(bf16[1,4096,2048]{2,1,0:T(8,128)(2,1)} %param.7, bf16[32,2048]{1,0:T(8,128)(2,1)S(1)} %collective-permute-done.44, bf16[32,2048]{1,0:T(8,128)(2,1)S(1)} %collective-permute-done.43, bf16[32,2048]{1,0:T(8,128)(2,1)S(1)} %collective-permute-done.42, bf16[32,2048]{1,0:T(8,128)(2,1)S(1)} %get-tuple-element.96), kind=kOutput, calls=%fused_computation.46 | convolution fusion | flops 2150105088 | bytes 18350080 | tf_op jit(solution)/shard_map/dot_general | solution.py:37
  59.4 11.5 %fusion.58 = bf16[128,4096]{1,0:T(8,128)(2,1)S(1)} fusion(bf16[1,4096,2048]{2,1,0:T(8,128)(2,1)} %param.7, bf16[32,2048]{1,0:T(8,128)(2,1)S(1)} %collective-permute-done.65, bf16[32,2048]{1,0:T(8,128)(2,1)S(1)} %collective-permute-done.64, bf16[32,2048]{1,0:T(8,128)(2,1)} %copy-done.45, bf16[32,2048]{1,0:T(8,128)(2,1)S(1)} %get-tuple-element.93), kind=kOutput, calls=%fused_computation.48 | convolution fusion | flops 2150105088 | bytes 18350080 | tf_op jit(solution)/shard_map/dot_general | solution.py:37
  73.5 11.5 %fusion.46 = bf16[128,4096]{1,0:T(8,128)(2,1)S(1)} fusion(bf16[1,4096,2048]{2,1,0:T(8,128)(2,1)} %param.7, bf16[32,2048]{1,0:T(8,128)(2,1)S(1)} %collective-permute-done.23, bf16[32,2048]{1,0:T(8,128)(2,1)} %copy-done.43, bf16[32,2048]{1,0:T(8,128)(2,1)} %copy-done.44, bf16[32,2048]{1,0:T(8,128)(2,1)S(1)} %get-tuple-element.94), kind=kOutput, calls=%fused_computation.44 | convolution fusion | flops 2150105088 | bytes 18350080 | tf_op jit(solution)/shard_map/dot_general | solution.py:37
  86.5 12.6 %fusion.40 = bf16[128,4096]{1,0:T(8,128)(2,1)} fusion(bf16[1,4096,2048]{2,1,0:T(8,128)(2,1)} %param.7, bf16[32,2048]{1,0:T(8,128)(2,1)} %collective-permute-done.2, bf16[32,2048]{1,0:T(8,128)(2,1)} %collective-permute-done.1, bf16[32,2048]{1,0:T(8,128)(2,1)} %collective-permute-done, bf16[32,2048]{1,0:T(8,128)(2,1)S(1)} %get-tuple-element.95), kind=kOutput, calls=%fused_computation.42 | convolution fusion | flops 2150105088 | bytes 18350080 | tf_op jit(solution)/shard_map/dot_general | solution.py:37
  122.7 32.2 %collective-permute-done.67 = bf16[128,2048]{1,0:T(8,128)(2,1)S(1)} collective-permute-done((bf16[128,2048]{1,0:T(8,128)(2,1)S(1)}, bf16[128,2048]{1,0:T(8,128)(2,1)S(1)}, u32[]{:S(2)}, u32[]{:S(2)}) %collective-permute-start.67) | collective-permute-done | bytes 524320 | tf_op jit(solution)/shard_map/ppermute | solution.py:13
  167.6 21.0 %collective-permute-done.25 = bf16[128,2048]{1,0:T(8,128)(2,1)S(1)} collective-permute-done((bf16[128,2048]{1,0:T(8,128)(2,1)S(1)}, bf16[128,2048]{1,0:T(8,128)(2,1)S(1)}, u32[]{:S(2)}, u32[]{:S(2)}) %collective-permute-start.25) | collective-permute-done | bytes 524320 | tf_op jit(solution)/shard_map/ppermute | solution.py:13
  189.6 9.5 %collective-permute-done.4 = bf16[128,2048]{1,0:T(8,128)(2,1)S(1)} collective-permute-done((bf16[128,2048]{1,0:T(8,128)(2,1)S(1)}, bf16[128,2048]{1,0:T(8,128)(2,1)S(1)}, u32[]{:S(2)}, u32[]{:S(2)}) %collective-permute-start.4) | collective-permute-done | bytes 524320 | tf_op jit(solution)/shard_map/ppermute | solution.py:13
  200.1 11.4 %fusion.124 = bf16[128,2048]{1,0:T(8,128)(2,1)S(1)} fusion(bf16[1,2048,4096]{2,1,0:T(8,128)(2,1)} %param.6, bf16[128,2048]{1,0:T(8,128)(2,1)S(1)} %get-tuple-element.68, bf16[128,2048]{1,0:T(8,128)(2,1)S(1)} %get-tuple-element.67), kind=kOutput, calls=%fused_computation.90 | convolution fusion | flops 2149842944 | bytes 18350080 | tf_op jit(solution)/shard_map/dot_general | solution.py:37
  217.7 11.4 %fusion.112 = bf16[128,2048]{1,0:T(8,128)(2,1)S(1)} fusion(bf16[1,2048,4096]{2,1,0:T(8,128)(2,1)} %param.6, bf16[128,2048]{1,0:T(8,128)(2,1)S(1)} %get-tuple-element.72, bf16[128,2048]{1,0:T(8,128)(2,1)S(1)} %get-tuple-element.71), kind=kOutput, calls=%fused_computation.86 | convolution fusion | flops 2149842944 | bytes 18350080 | tf_op jit(solution)/shard_map/dot_general | solution.py:37
  235.2 11.6 %fusion.106 = bf16[128,2048]{1,0:T(8,128)(2,1)S(1)} fusion(bf16[1,2048,4096]{2,1,0:T(8,128)(2,1)} %param.6, bf16[128,2048]{1,0:T(8,128)(2,1)} %get-tuple-element.74, bf16[128,2048]{1,0:T(8,128)(2,1)S(1)} %get-tuple-element.73), kind=kOutput, calls=%fused_computation.84 | convolution fusion | flops 2149842944 | bytes 18350080 | tf_op jit(solution)/shard_map/dot_general | solution.py:37
  255.5 11.6 %fusion.118 = bf16[128,2048]{1,0:T(8,128)(2,1)S(1)} fusion(bf16[1,2048,4096]{2,1,0:T(8,128)(2,1)} %param.6, bf16[128,2048]{1,0:T(8,128)(2,1)} %get-tuple-element.70, bf16[128,2048]{1,0:T(8,128)(2,1)S(1)} %get-tuple-element.69), kind=kOutput, calls=%fused_computation.88 | convolution fusion | flops 2149842944 | bytes 18350080 | tf_op jit(solution)/shard_map/dot_general | solution.py:37
  309.7 11.4 %fusion.43 = bf16[128,4096]{1,0:T(8,128)(2,1)S(1)} fusion(bf16[1,4096,2048]{2,1,0:T(8,128)(2,1)} %param.7, bf16[32,2048]{1,0:T(8,128)(2,1)S(1)} %collective-permute-done.14, bf16[32,2048]{1,0:T(8,128)(2,1)S(1)} %collective-permute-done.13, bf16[32,2048]{1,0:T(8,128)(2,1)S(1)} %collective-permute-done.12, bf16[32,2048]{1,0:T(8,128)(2,1)S(1)} %get-tuple-element.10), kind=kOutput, calls=%fused_computation.43 | convolution fusion | flops 2150105088 | bytes 18350080 | tf_op jit(solution)/shard_map/dot_general | solution.py:37
  329.1 11.5 %fusion.49 = bf16[128,4096]{1,0:T(8,128)(2,1)S(1)} fusion(bf16[1,4096,2048]{2,1,0:T(8,128)(2,1)} %param.7, bf16[32,2048]{1,0:T(8,128)(2,1)S(1)} %collective-permute-done.35, bf16[32,2048]{1,0:T(8,128)(2,1)S(1)} %collective-permute-done.34, bf16[32,2048]{1,0:T(8,128)(2,1)} %copy-done.35, bf16[32,2048]{1,0:T(8,128)(2,1)S(1)} %get-tuple-element.8), kind=kOutput, calls=%fused_computation.45 | convolution fusion | flops 2150105088 | bytes 18350080 | tf_op jit(solution)/shard_map/dot_general | solution.py:37
  350.5 11.6 %fusion.55 = bf16[128,4096]{1,0:T(8,128)(2,1)S(1)} fusion(bf16[1,4096,2048]{2,1,0:T(8,128)(2,1)} %param.7, bf16[32,2048]{1,0:T(8,128)(2,1)} %copy-done.33, bf16[32,2048]{1,0:T(8,128)(2,1)} %copy-done.34, bf16[32,2048]{1,0:T(8,128)(2,1)} %collective-permute-done.54, bf16[32,2048]{1,0:T(8,128)(2,1)S(1)} %get-tuple-element.6), kind=kOutput, calls=%fused_computation.47 | convolution fusion | flops 2150105088 | bytes 18350080 | tf_op jit(solution)/shard_map/dot_general | solution.py:37
  363.0 12.6 %fusion.61 = bf16[128,4096]{1,0:T(8,128)(2,1)} fusion(bf16[1,4096,2048]{2,1,0:T(8,128)(2,1)} %param.7, bf16[32,2048]{1,0:T(8,128)(2,1)} %collective-permute-done.77, bf16[32,2048]{1,0:T(8,128)(2,1)} %collective-permute-done.76, bf16[32,2048]{1,0:T(8,128)(2,1)} %collective-permute-done.75, bf16[32,2048]{1,0:T(8,128)(2,1)S(1)} %get-tuple-element.4), kind=kOutput, calls=%fused_computation.49 | convolution fusion | flops 2150105088 | bytes 18350080 | tf_op jit(solution)/shard_map/dot_general | solution.py:37
  399.9 9.7 %collective-permute-done.37 = bf16[128,2048]{1,0:T(8,128)(2,1)S(1)} collective-permute-done((bf16[128,2048]{1,0:T(8,128)(2,1)S(1)}, bf16[128,2048]{1,0:T(8,128)(2,1)S(1)}, u32[]{:S(2)}, u32[]{:S(2)}) %collective-permute-start.37) | collective-permute-done | bytes 524320 | tf_op jit(solution)/shard_map/ppermute | solution.py:13
  411.3 9.5 %collective-permute-done.58 = bf16[128,2048]{1,0:T(8,128)(2,1)S(1)} collective-permute-done((bf16[128,2048]{1,0:T(8,128)(2,1)S(1)}, bf16[128,2048]{1,0:T(8,128)(2,1)S(1)}, u32[]{:S(2)}, u32[]{:S(2)}) %collective-permute-start.58) | collective-permute-done | bytes 524320 | tf_op jit(solution)/shard_map/ppermute | solution.py:13
  433.1 11.4 %fusion.109 = bf16[128,2048]{1,0:T(8,128)(2,1)S(1)} fusion(bf16[1,2048,4096]{2,1,0:T(8,128)(2,1)} %param.6, bf16[128,2048]{1,0:T(8,128)(2,1)S(1)} %get-tuple-element.60, bf16[128,2048]{1,0:T(8,128)(2,1)S(1)} %get-tuple-element.59), kind=kOutput, calls=%fused_computation.85 | convolution fusion | flops 2149842944 | bytes 18350080 | tf_op jit(solution)/shard_map/dot_general | solution.py:37
  452.9 11.4 %fusion.115 = bf16[128,2048]{1,0:T(8,128)(2,1)S(1)} fusion(bf16[1,2048,4096]{2,1,0:T(8,128)(2,1)} %param.6, bf16[128,2048]{1,0:T(8,128)(2,1)S(1)} %get-tuple-element.62, bf16[128,2048]{1,0:T(8,128)(2,1)S(1)} %get-tuple-element.61), kind=kOutput, calls=%fused_computation.87 | convolution fusion | flops 2149842944 | bytes 18350080 | tf_op jit(solution)/shard_map/dot_general | solution.py:37
  474.8 12.3 %fusion.121 = bf16[128,2048]{1,0:T(8,128)(2,1)} fusion(bf16[1,2048,4096]{2,1,0:T(8,128)(2,1)} %param.6, bf16[128,2048]{1,0:T(8,128)(2,1)S(1)} %get-tuple-element.64, bf16[128,2048]{1,0:T(8,128)(2,1)S(1)} %get-tuple-element.63), kind=kOutput, calls=%fused_computation.89 | convolution fusion | flops 2149842944 | bytes 18350080 | tf_op jit(solution)/shard_map/dot_general | solution.py:37
  498.0 12.6 %fusion.127 = bf16[128,2048]{1,0:T(8,128)(2,1)} fusion(bf16[1,2048,4096]{2,1,0:T(8,128)(2,1)} %param.6, bf16[128,2048]{1,0:T(8,128)(2,1)} %get-tuple-element.66, bf16[128,2048]{1,0:T(8,128)(2,1)} %get-tuple-element.65), kind=kOutput, calls=%fused_computation.91 | convolution fusion | flops 2149842944 | bytes 18350080 | tf_op jit(solution)/shard_map/dot_general | solution.py:37
  515.3 16.6 %convert_bitcast_fusion.1 = bf16[1,2048,4096]{2,1,0:T(8,128)(2,1)} fusion(bf16[512,2048]{1,0:T(8,128)(2,1)} %copy-done.46, bf16[128,2048]{1,0:T(8,128)(2,1)} %get-tuple-element.66, bf16[128,2048]{1,0:T(8,128)(2,1)} %get-tuple-element.65, bf16[128,2048]{1,0:T(8,128)(2,1)S(1)} %get-tuple-element.64, bf16[128,2048]{1,0:T(8,128)(2,1)S(1)} %get-tuple-element.63, ...), kind=kOutput, calls=%fused_computation.41 | convolution fusion | flops 8631877632 | bytes 23068672 | tf_op jit(solution)/shard_map/dot_general | solution.py:31
  533.9 27.4 %convert_bitcast_fusion = bf16[1,4096,2048]{2,1,0:T(8,128)(2,1)} fusion(bf16[512,2048]{1,0:T(8,128)(2,1)} %constant_dynamic-update-slice_fusion.16, bf16[128,2048]{1,0:T(8,128)(2,1)S(1)} %get-tuple-element.56, bf16[128,2048]{1,0:T(8,128)(2,1)S(1)} %get-tuple-element.55, bf16[128,2048]{1,0:T(8,128)(2,1)} %get-tuple-element.52, ...), kind=kOutput, calls=%fused_computation.40 | convolution fusion | flops 8631877632 | bytes 23068672 | tf_op jit(solution)/shard_map/dot_general | solution.py:31
  (369 shorter events, 248.5 us)
Async XLA Ops:
  1.9 51.8 %collective-permute-start.65 = (bf16[32,2048]{1,0:T(8,128)(2,1)S(1)}, bf16[32,2048]{1,0:T(8,128)(2,1)S(1)}, u32[]{:S(2)}, u32[]{:S(2)}) collective-permute-start(bf16[32,2048]{1,0:T(8,128)(2,1)S(1)} %get-tuple-element.93), channel_id=1, source_target_pairs={{0,12},{4,0},{8,4},{12,8},{1,13},{5,1},{9,5},{13,9},{2,14},{6,2},{... | collective-permute-start | bytes 393224 | tf_op jit(solution)/shard_map/ppermute | solution.py:13
  7.0 47.4 %collective-permute-start.64 = (bf16[32,2048]{1,0:T(8,128)(2,1)S(1)}, bf16[32,2048]{1,0:T(8,128)(2,1)S(1)}, u32[]{:S(2)}, u32[]{:S(2)}) collective-permute-start(bf16[32,2048]{1,0:T(8,128)(2,1)S(1)} %get-tuple-element.93), channel_id=1, source_target_pairs={{0,8},{4,12},{8,0},{12,4},{1,9},{5,13},{9,1},{13,5},{2,10},{6,14},... | collective-permute-start | bytes 393224 | tf_op jit(solution)/shard_map/ppermute | solution.py:13
  109.2 48.0 %collective-permute-start.48 = (bf16[128,2048]{1,0:T(8,128)(2,1)S(1)}, bf16[128,2048]{1,0:T(8,128)(2,1)S(1)}, u32[]{:S(2)}, u32[]{:S(2)}) collective-permute-start(bf16[128,2048]{1,0:T(8,128)(2,1)S(1)} %add_convert_fusion.4), channel_id=1, source_target_pairs={{0,2},{1,3},{2,0},{3,1},{4,6},{5,7},{6,4},{7,5},{8,10},{9,11},{10,... | collective-permute-start | bytes 1572872 | tf_op jit(solution)/shard_map/ppermute | solution.py:13
  110.1 56.9 %collective-permute-start.27 = (bf16[128,2048]{1,0:T(8,128)(2,1)S(1)}, bf16[128,2048]{1,0:T(8,128)(2,1)S(1)}, u32[]{:S(2)}, u32[]{:S(2)}) collective-permute-start(bf16[128,2048]{1,0:T(8,128)(2,1)S(1)} %add_convert_fusion.7), channel_id=1, source_target_pairs={{0,2},{1,3},{2,0},{3,1},{4,6},{5,7},{6,4},{7,5},{8,10},{9,11},{10,... | collective-permute-start | bytes 1572872 | tf_op jit(solution)/shard_map/ppermute | solution.py:13
  111.9 43.0 %collective-permute-start.67 = (bf16[128,2048]{1,0:T(8,128)(2,1)S(1)}, bf16[128,2048]{1,0:T(8,128)(2,1)S(1)}, u32[]{:S(2)}, u32[]{:S(2)}) collective-permute-start(bf16[128,2048]{1,0:T(8,128)(2,1)S(1)} %add_convert_fusion.2), channel_id=1, source_target_pairs={{0,2},{1,3},{2,0},{3,1},{4,6},{5,7},{6,4},{7,5},{8,10},{9,11},{10,... | collective-permute-start | bytes 1572872 | tf_op jit(solution)/shard_map/ppermute | solution.py:13
  112.8 53.3 %collective-permute-start.46 = (bf16[128,2048]{1,0:T(8,128)(2,1)S(1)}, bf16[128,2048]{1,0:T(8,128)(2,1)S(1)}, u32[]{:S(2)}, u32[]{:S(2)}) collective-permute-start(bf16[128,2048]{1,0:T(8,128)(2,1)S(1)} %add_convert_fusion.5), channel_id=1, source_target_pairs={{0,2},{1,3},{2,0},{3,1},{4,6},{5,7},{6,4},{7,5},{8,10},{9,11},{10,... | collective-permute-start | bytes 1572872 | tf_op jit(solution)/shard_map/ppermute | solution.py:13
  121.2 68.4 %collective-permute-start.6 = (bf16[128,2048]{1,0:T(8,128)(2,1)S(1)}, bf16[128,2048]{1,0:T(8,128)(2,1)S(1)}, u32[]{:S(2)}, u32[]{:S(2)}) collective-permute-start(bf16[128,2048]{1,0:T(8,128)(2,1)S(1)} %add_convert_fusion.10), channel_id=1, source_target_pairs={{0,2},{1,3},{2,0},{3,1},{4,6},{5,7},{6,4},{7,5},{8,10},{9,11},{10,... | collective-permute-start | bytes 1572872 | tf_op jit(solution)/shard_map/ppermute | solution.py:13
  157.3 41.8 %collective-permute-start.4 = (bf16[128,2048]{1,0:T(8,128)(2,1)S(1)}, bf16[128,2048]{1,0:T(8,128)(2,1)S(1)}, u32[]{:S(2)}, u32[]{:S(2)}) collective-permute-start(bf16[128,2048]{1,0:T(8,128)(2,1)S(1)} %add_convert_fusion.11), channel_id=1, source_target_pairs={{0,2},{1,3},{2,0},{3,1},{4,6},{5,7},{6,4},{7,5},{8,10},{9,11},{10,... | collective-permute-start | bytes 1572872 | tf_op jit(solution)/shard_map/ppermute | solution.py:13
  167.0 79.8 %collective-permute-start.49 = (bf16[128,2048]{1,0:T(8,128)(2,1)S(1)}, bf16[128,2048]{1,0:T(8,128)(2,1)}, u32[]{:S(2)}, u32[]{:S(2)}) collective-permute-start(bf16[128,2048]{1,0:T(8,128)(2,1)S(1)} %multiply_convert_fusion.7), channel_id=1, source_target_pairs={{0,1},{1,0},{2,3},{3,2},{4,5},{5,4},{6,7},{7,6},{8,9},{9,8},{10,11... | collective-permute-start | bytes 1572872 | tf_op jit(solution)/shard_map/ppermute | solution.py:18
  212.3 37.9 %collective-permute-start.71 = (bf16[32,2048]{1,0:T(8,128)(2,1)}, bf16[32,2048]{1,0:T(8,128)(2,1)S(1)}, u32[]{:S(2)}, u32[]{:S(2)}) collective-permute-start(bf16[32,2048]{1,0:T(8,128)(2,1)} %get-tuple-element.90), channel_id=1, source_target_pairs={{0,12},{4,0},{8,4},{12,8},{1,13},{5,1},{9,5},{13,9},{2,14},{6,2},{... | collective-permute-start | bytes 393224 | tf_op jit(solution)/shard_map/ppermute | solution.py:13
  216.0 35.6 %collective-permute-start.73 = (bf16[32,2048]{1,0:T(8,128)(2,1)}, bf16[32,2048]{1,0:T(8,128)(2,1)S(1)}, u32[]{:S(2)}, u32[]{:S(2)}) collective-permute-start(bf16[32,2048]{1,0:T(8,128)(2,1)} %get-tuple-element.91), channel_id=1, source_target_pairs={{0,4},{4,8},{8,12},{12,0},{1,5},{5,9},{9,13},{13,1},{2,6},{6,10},{... | collective-permute-start | bytes 393224 | tf_op jit(solution)/shard_map/ppermute | solution.py:13
  216.0 38.5 %collective-permute-start.72 = (bf16[32,2048]{1,0:T(8,128)(2,1)}, bf16[32,2048]{1,0:T(8,128)(2,1)S(1)}, u32[]{:S(2)}, u32[]{:S(2)}) collective-permute-start(bf16[32,2048]{1,0:T(8,128)(2,1)} %get-tuple-element.92), channel_id=1, source_target_pairs={{0,8},{4,12},{8,0},{12,4},{1,9},{5,13},{9,1},{13,5},{2,10},{6,14},... | collective-permute-start | bytes 393224 | tf_op jit(solution)/shard_map/ppermute | solution.py:13
  291.9 52.5 %collective-permute-start.74 = (bf16[32,2048]{1,0:T(8,128)(2,1)}, bf16[32,2048]{1,0:T(8,128)(2,1)}, u32[]{:S(2)}, u32[]{:S(2)}) collective-permute-start(bf16[32,2048]{1,0:T(8,128)(2,1)} %get-tuple-element.87), channel_id=1, source_target_pairs={{16,0},{17,1},{18,2},{19,3},{20,4},{21,5},{22,6},{23,7},{24,8},{25... | collective-permute-start | bytes 393224 | tf_op jit(solution)/shard_map/ppermute | solution.py:111
  322.0 60.2 %collective-permute-start.15 = (bf16[128,2048]{1,0:T(8,128)(2,1)}, bf16[128,2048]{1,0:T(8,128)(2,1)}, u32[]{:S(2)}, u32[]{:S(2)}) collective-permute-start(bf16[128,2048]{1,0:T(8,128)(2,1)} %broadcast_select_fusion.31), channel_id=1, source_target_pairs={{0,1},{1,0},{2,3},{3,2},{4,5},{5,4},{6,7},{7,6},{8,9},{9,8},{10,11... | collective-permute-start | bytes 1572872 | tf_op jit(solution)/shard_map/ppermute | solution.py:18
  341.4 43.6 %collective-permute-start.36 = (bf16[128,2048]{1,0:T(8,128)(2,1)}, bf16[128,2048]{1,0:T(8,128)(2,1)}, u32[]{:S(2)}, u32[]{:S(2)}) collective-permute-start(bf16[128,2048]{1,0:T(8,128)(2,1)} %broadcast_select_fusion.24), channel_id=1, source_target_pairs={{0,1},{1,0},{2,3},{3,2},{4,5},{5,4},{6,7},{7,6},{8,9},{9,8},{10,11... | collective-permute-start | bytes 1572872 | tf_op jit(solution)/shard_map/ppermute | solution.py:18
  390.1 41.0 %collective-permute-start.79 = (bf16[128,2048]{1,0:T(8,128)(2,1)S(1)}, bf16[128,2048]{1,0:T(8,128)(2,1)S(1)}, u32[]{:S(2)}, u32[]{:S(2)}) collective-permute-start(bf16[128,2048]{1,0:T(8,128)(2,1)S(1)} %add_convert_fusion), channel_id=1, source_target_pairs={{0,2},{1,3},{2,0},{3,1},{4,6},{5,7},{6,4},{7,5},{8,10},{9,11},{10,... | collective-permute-start | bytes 1572872 | tf_op jit(solution)/shard_map/ppermute | solution.py:13
  399.3 49.3 %collective-permute-start.84 = (bf16[128,2048]{1,0:T(8,128)(2,1)S(1)}, bf16[128,2048]{1,0:T(8,128)(2,1)}, u32[]{:S(2)}, u32[]{:S(2)}) collective-permute-start(bf16[128,2048]{1,0:T(8,128)(2,1)S(1)} %get-tuple-element.45), channel_id=1, source_target_pairs={{0,1},{1,0},{2,3},{3,2},{4,5},{5,4},{6,7},{7,6},{8,9},{9,8},{10,11... | collective-permute-start | bytes 1572872 | tf_op jit(solution)/shard_map/ppermute | solution.py:18
  411.3 59.0 %collective-permute-start.85 = (bf16[128,2048]{1,0:T(8,128)(2,1)}, bf16[128,2048]{1,0:T(8,128)(2,1)}, u32[]{:S(2)}, u32[]{:S(2)}) collective-permute-start(bf16[128,2048]{1,0:T(8,128)(2,1)} %get-tuple-element.49), channel_id=1, source_target_pairs={{0,1},{1,0},{2,3},{3,2},{4,5},{5,4},{6,7},{7,6},{8,9},{9,8},{10,11... | collective-permute-start | bytes 1572872 | tf_op jit(solution)/shard_map/ppermute | solution.py:18
  431.1 62.6 %collective-permute-start.86 = (bf16[128,2048]{1,0:T(8,128)(2,1)}, bf16[128,2048]{1,0:T(8,128)(2,1)}, u32[]{:S(2)}, u32[]{:S(2)}) collective-permute-start(bf16[128,2048]{1,0:T(8,128)(2,1)} %get-tuple-element.53), channel_id=1, source_target_pairs={{0,1},{1,0},{2,3},{3,2},{4,5},{5,4},{6,7},{7,6},{8,9},{9,8},{10,11... | collective-permute-start | bytes 1572872 | tf_op jit(solution)/shard_map/ppermute | solution.py:18
  465.1 66.8 %collective-permute-start.87 = (bf16[128,2048]{1,0:T(8,128)(2,1)}, bf16[128,2048]{1,0:T(8,128)(2,1)}, u32[]{:S(2)}, u32[]{:S(2)}) collective-permute-start(bf16[128,2048]{1,0:T(8,128)(2,1)} %get-tuple-element.57), channel_id=1, source_target_pairs={{0,1},{1,0},{2,3},{3,2},{4,5},{5,4},{6,7},{7,6},{8,9},{9,8},{10,11... | collective-permute-start | bytes 1572872 | tf_op jit(solution)/shard_map/ppermute | solution.py:18
  488.9 72.4 %collective-permute-start.60 = (bf16[32,2048]{1,0:T(8,128)(2,1)}, bf16[32,2048]{1,0:T(8,128)(2,1)}, u32[]{:S(2)}, u32[]{:S(2)}) collective-permute-start(bf16[32,2048]{1,0:T(8,128)(2,1)} %get-tuple-element.81), channel_id=1, source_target_pairs={{0,12},{4,0},{8,4},{12,8},{1,13},{5,1},{9,5},{13,9},{2,14},{6,2},{... | collective-permute-start | bytes 393224 | tf_op jit(solution)/shard_map/ppermute | solution.py:13
  491.8 71.1 %collective-permute-start.62 = (bf16[32,2048]{1,0:T(8,128)(2,1)}, bf16[32,2048]{1,0:T(8,128)(2,1)}, u32[]{:S(2)}, u32[]{:S(2)}) collective-permute-start(bf16[32,2048]{1,0:T(8,128)(2,1)} %get-tuple-element.82), channel_id=1, source_target_pairs={{0,4},{4,8},{8,12},{12,0},{1,5},{5,9},{9,13},{13,1},{2,6},{6,10},{... | collective-permute-start | bytes 393224 | tf_op jit(solution)/shard_map/ppermute | solution.py:13
  493.7 69.2 %collective-permute-start.61 = (bf16[32,2048]{1,0:T(8,128)(2,1)}, bf16[32,2048]{1,0:T(8,128)(2,1)}, u32[]{:S(2)}, u32[]{:S(2)}) collective-permute-start(bf16[32,2048]{1,0:T(8,128)(2,1)} %get-tuple-element.83), channel_id=1, source_target_pairs={{0,8},{4,12},{8,0},{12,4},{1,9},{5,13},{9,1},{13,5},{2,10},{6,14},... | collective-permute-start | bytes 393224 | tf_op jit(solution)/shard_map/ppermute | solution.py:13
  512.4 51.7 %collective-permute-start.81 = (bf16[32,2048]{1,0:T(8,128)(2,1)}, bf16[32,2048]{1,0:T(8,128)(2,1)}, u32[]{:S(2)}, u32[]{:S(2)}) collective-permute-start(bf16[32,2048]{1,0:T(8,128)(2,1)} %get-tuple-element.84), channel_id=1, source_target_pairs={{0,12},{4,0},{8,4},{12,8},{1,13},{5,1},{9,5},{13,9},{2,14},{6,2},{... | collective-permute-start | bytes 393224 | tf_op jit(solution)/shard_map/ppermute | solution.py:13
  (115 other events, 2039.2 us)

commit v2 on v1

v2 whole, which is shorter than its diff:
```python
import jax
import jax.numpy as jnp
from jax import lax
from jax.experimental.layout import Layout, with_layout_constraint
from jax.sharding import PartitionSpec as P

gelu_scale = 0.7978845608028654
cubic_term = 0.044715
CHUNK_ROWS = 64


def shifted(block, axis, distance):
    size = lax.axis_size(axis)
    return lax.ppermute(block, axis, [(i, (i + distance) % size) for i in range(size)])


def from_partner(block):
    size = lax.axis_size("narrow")
    return lax.ppermute(block, "narrow", [(i, i ^ 1) for i in range(size)])


def gelu_parts(pre_act):
    inner = jnp.tanh(gelu_scale * (pre_act + cubic_term * pre_act * pre_act * pre_act))
    act_value = 0.5 * pre_act * (1.0 + inner)
    slopes = 0.5 * (1.0 + inner) + 0.5 * pre_act * (1.0 - inner * inner) * gelu_scale * (
        1.0 + 3.0 * cubic_term * pre_act * pre_act
    )
    return (act_value, slopes)


def contract(first_op, second_op, dims):
    return lax.dot_general(
        first_op, second_op, ((dims[:1], dims[1:]), ((), ())), preferred_element_type=jnp.float32
    )


def row_major(block):
    return with_layout_constraint(block, Layout(major_to_minor=(0, 1)))


def turned(block):
    return row_major(block.T)


def sum_half(part, axis, is_odd):
    low, high = jnp.split(part, 2, axis=axis)
    got = from_partner(jnp.where(is_odd, low, high))
    mine = jnp.where(is_odd, high, low)
    chip = (mine.astype(jnp.float32) + got.astype(jnp.float32)).astype(jnp.bfloat16)
    total = chip.astype(jnp.float32)
    for step in range(1, lax.axis_size("narrow") // 2):
        total = total + shifted(chip, "narrow", 2 * step).astype(jnp.float32)
    return total


def both_halves(mine, axis, is_odd):
    other = from_partner(mine)
    return jnp.concatenate(
        [jnp.where(is_odd, other, mine), jnp.where(is_odd, mine, other)], axis=axis
    )


def wide_masks():
    size = lax.axis_size("wide")
    return [1 << bit for bit in range(size.bit_length() - 1)]


def from_place(block, mask):
    return lax.ppermute(
        block, "wide", [(i, i ^ mask) for i in range(lax.axis_size("wide"))]
    )


def block_order():
    order = [0]
    for mask in reversed(wide_masks()):
        order = order + [j ^ mask for j in order]
    return order


def gather_wide(rows):
    for mask in reversed(wide_masks()):
        rows = jnp.concatenate([rows, from_place(rows, mask)], axis=0)
    return rows


def scatter_wide(part, own_rows):
    for mask in wide_masks():
        keep, send = jnp.split(part, 2, axis=0)
        total = keep.astype(jnp.float32) + from_place(send, mask).astype(jnp.float32)
        part = total.astype(jnp.bfloat16)
    return (own_rows.astype(jnp.float32) + total).astype(jnp.bfloat16)


def body(saved_inputs, upstream, up_weight, down_weight):
    w_up = up_weight[0]
    w_down = down_weight[0]
    wide = lax.axis_size("wide")
    place = lax.axis_index("wide")
    is_odd = lax.axis_index("narrow") % 2 == 1
    is_upper = lax.axis_index("section") == 1
    tokens, width = saved_inputs.shape[1:]
    rows = min(CHUNK_ROWS, tokens // wide)
    chunks = tokens // wide // rows

    blocks = saved_inputs[0].reshape(wide, chunks, rows, width)
    blocks = [
        lax.dynamic_index_in_dim(blocks, jnp.bitwise_xor(place, j), 0, keepdims=False)
        for j in block_order()
    ]
    saved = [
        jnp.concatenate([block[c] for block in blocks], axis=0) for c in range(chunks)
    ]
    own = [upstream[c * rows : (c + 1) * rows] for c in range(chunks)]

    def backward(incoming, own_rows, slopes):
        part = row_major(contract(w_down, turned(incoming), (1, 0)).astype(jnp.bfloat16))
        back = sum_half(part, 0, is_odd)
        slope = row_major(both_halves((back * slopes).astype(jnp.bfloat16), 0, is_odd))
        part = row_major(contract(w_up, slope, (1, 0)).astype(jnp.bfloat16))
        return slope, scatter_wide(turned(part), own_rows)

    hidden, slopes, second = [], [], []
    for c in range(chunks):
        first_in = gather_wide(own[c])
        part = contract(saved[c], w_up, (1, 0)).astype(jnp.bfloat16)
        act, slope_of = gelu_parts(sum_half(part, 1, is_odd))
        hidden.append(both_halves(act.astype(jnp.bfloat16), 1, is_odd))
        slopes.append(turned(slope_of))
        _, grad = backward(first_in, own[c], slopes[c])
        second.append(lax.ppermute(grad, "section", [(1, 0)]))
    incoming, slope, grads = [], [], []
    for c in range(chunks):
        own_rows = jnp.where(is_upper, own[c], second[c])
        incoming.append(gather_wide(own_rows))
        one_slope, grad = backward(incoming[c], own_rows, slopes[c])
        slope.append(one_slope)
        grads.append(grad)
    grad_down = contract(
        jnp.concatenate(hidden, axis=0), jnp.concatenate(incoming, axis=0), (0, 0)
    ).astype(jnp.bfloat16)
    grad_up = contract(
        jnp.concatenate(saved, axis=0), jnp.concatenate(slope, axis=1), (0, 1)
    ).astype(jnp.bfloat16)
    return jnp.concatenate(grads, axis=0)[None], grad_up[None], grad_down[None]


def solution(mesh):
    placed = (
        P("section", None, "narrow"),
        P("wide", "narrow"),
        P("section", "narrow", "wide"),
        P("section", "wide", "narrow"),
    )
    return jax.shard_map(
        body,
        mesh=mesh,
        in_specs=placed,
        out_specs=(
            P("section", "wide", "narrow"),
            P("section", "narrow", "wide"),
            P("section", "wide", "narrow"),
        ),
        check_vma=False,
    )
```

time: 582 us -> 451 us (0.77)
  matrix products: 248 us -> 134 us
  waiting for transfers between devices: 141 us -> 228 us
  starting transfers between devices: 93 us -> 28.6 us
  other arithmetic: 60.4 us -> 30 us
    dot_general x22 -> x12, matrix products: 248 us -> 134 us  [contract(): lax.dot_general(first_op, second_op, ((dims[:1], dims[1:]), ((), ())), pr...]
    ppermute x0 -> x16, waiting for transfers between devices: none -> 91.4 us  [from_place(): lax.ppermute(block, 'wide', [(i, i ^ mask) for i in range(lax.axis_size('...]
    ppermute x60 -> x6, starting transfers between devices: 83.3 us -> 6.62 us  [shifted(): lax.ppermute(block, axis, [(i, (i + distance) % size) for i in range(size)])]
    ppermute x0 -> x16, starting transfers between devices: none -> 18.2 us  [from_place(): lax.ppermute(block, 'wide', [(i, i ^ mask) for i in range(lax.axis_size('...]
    ppermute x60 -> x6, waiting for transfers between devices: 138 us -> 128 us  [shifted(): lax.ppermute(block, axis, [(i, (i + distance) % size) for i in range(size)])]
    select_n x12 -> x6, other arithmetic: 15.3 us -> 6.31 us  [both_halves(): jnp.where(is_odd, other, mine)]
    select_n x12 -> x6, other arithmetic: 10.7 us -> 2.27 us  [sum_half(): got = from_partner(jnp.where(is_odd, low, high))]
    convert_element_type x12 -> x6, other arithmetic: 10.5 us -> 2.36 us  [sum_half(): (mine.astype(jnp.float32) + got.astype(jnp.float32)).astype(jnp.bfloat16)]
  transfers between devices with their start and end apart: 88 -> 36, of which waited for: 16 -> 15; matrix products, arithmetic and copies ran while one was open for 57% -> 40% of each run, Pallas kernels for 0% -> 0%
where the time goes in v2:
time: 451 us; the launch traced here: 447 us
  waiting for transfers between devices  228 us (51%)
  matrix products  134 us (30%)
  other arithmetic  30 us (7%)
  starting transfers between devices  28.6 us (6%)
  local copies, waits for them, and re-layouts  24.9 us (6%)
    dot_general x12, matrix products, contract(): lax.dot_general(first_op, second_op, ((dims[:1], dims[1:]), ((), ())), pr...  134 us
    ppermute x6, waiting for transfers between devices, shifted(): lax.ppermute(block, axis, [(i, (i + distance) % size) for i in range(size)])  128 us
    ppermute x16, waiting for transfers between devices, from_place(): lax.ppermute(block, 'wide', [(i, i ^ mask) for i in range(lax.axis_size('...  91.4 us
    ppermute x16, starting transfers between devices, from_place(): lax.ppermute(block, 'wide', [(i, i ^ mask) for i in range(lax.axis_size('...  18.2 us
    unnamed x52, local copies, waits for them, and re-layouts  10.5 us
  transfers between devices with their start and end apart: 36, of which 15 were waited for; matrix products, arithmetic and copies ran while one was open for 40% of the time, Pallas kernels for 0%

profile of v2, /device:TPU:0, one launch (start us, length us, event | category | flops | bytes accessed | tf_op | source)
XLA Modules:
  0.0 447.2 jit_solution(2313495711720048392)
XLA Ops:
  13.1 10.6 %fusion.35 = bf16[256,4096]{0,1:T(8,128)(2,1)S(1)} fusion(bf16[1,2048,4096]{2,1,0:T(8,128)(2,1)} %param.6, bf16[64,2048]{1,0:T(8,128)(2,1)S(1)} %get-tuple-element.8, bf16[64,2048]{1,0:T(8,128)(2,1)S(1)} %get-tuple-element.10, bf16[64,2048]{1,0:T(8,128)(2,1)S(1)} %get-tuple-element.12, bf16[64,2048]{1,0:T(8,128)(2,1)S(1)} %get-tuple-element.14), kind=kOutput, calls=%fused_computation.27 | convolution fusion | flops 4300210176 | bytes 19922944 | tf_op jit(solution)/shard_map/dot_general | solution.py:32
  25.4 12.9 %fusion.32 = bf16[256,4096]{0,1:T(8,128)(2,1)S(1)} fusion(bf16[1,2048,4096]{2,1,0:T(8,128)(2,1)} %param.6, bf16[64,2048]{1,0:T(8,128)(2,1)} %get-tuple-element.16, bf16[64,2048]{1,0:T(8,128)(2,1)} %get-tuple-element.18, bf16[64,2048]{1,0:T(8,128)(2,1)} %get-tuple-element.20, bf16[64,2048]{1,0:T(8,128)(2,1)} %get-tuple-element.22), kind=kOutput, calls=%fused_computation.26 | convolution fusion | flops 4300210176 | bytes 19922944 | tf_op jit(solution)/shard_map/dot_general | solution.py:32
  43.1 11.5 %collective-permute-done.18 = bf16[128,2048]{1,0:T(8,128)(2,1)S(1)} collective-permute-done((bf16[128,2048]{1,0:T(8,128)(2,1)S(1)}, bf16[128,2048]{1,0:T(8,128)(2,1)S(1)}, u32[]{:S(2)}, u32[]{:S(2)}) %collective-permute-start.18) | collective-permute-done | bytes 524320 | tf_op jit(solution)/shard_map/ppermute | solution.py:69
  54.6 10.4 %fusion.44 = bf16[4096,256]{1,0:T(8,128)(2,1)S(1)} fusion(bf16[1,4096,2048]{2,1,0:T(8,128)(2,1)} %param.7, bf16[128,2048]{1,0:T(8,128)(2,1)S(1)} %collective-permute-done.18, bf16[64,2048]{1,0:T(8,128)(2,1)} %collective-permute-done.17, bf16[64,2048]{1,0:T(8,128)(2,1)} %get-tuple-element.37), kind=kOutput, calls=%fused_computation.30 | convolution fusion | flops 4299161600 | bytes 19922944 | tf_op jit(solution)/shard_map/dot_general | solution.py:32
  65.7 10.3 %fusion.38 = bf16[4096,256]{1,0:T(8,128)(2,1)S(1)} fusion(bf16[1,4096,2048]{2,1,0:T(8,128)(2,1)} %param.7, bf16[128,2048]{1,0:T(8,128)(2,1)S(1)} %collective-permute-done.1, bf16[64,2048]{1,0:T(8,128)(2,1)} %collective-permute-done, bf16[64,2048]{1,0:T(8,128)(2,1)S(1)} %get-tuple-element.38), kind=kOutput, calls=%fused_computation.28 | convolution fusion | flops 4299161600 | bytes 19922944 | tf_op jit(solution)/shard_map/dot_general | solution.py:32
  83.6 20.4 %collective-permute-done.22 = bf16[256,2048]{0,1:T(8,128)(2,1)S(1)} collective-permute-done((bf16[256,2048]{0,1:T(8,128)(2,1)S(1)}, bf16[256,2048]{0,1:T(8,128)(2,1)S(1)}, u32[]{:S(2)}, u32[]{:S(2)}) %collective-permute-start.22) | collective-permute-done | bytes 1048608 | tf_op jit(solution)/shard_map/ppermute | solution.py:14
  104.1 22.5 %collective-permute-done.20 = bf16[2048,256]{1,0:T(8,128)(2,1)S(1)} collective-permute-done((bf16[2048,256]{1,0:T(8,128)(2,1)S(1)}, bf16[2048,256]{1,0:T(8,128)(2,1)S(1)}, u32[]{:S(2)}, u32[]{:S(2)}) %collective-permute-start.20) | collective-permute-done | bytes 1048608 | tf_op jit(solution)/shard_map/ppermute | solution.py:14
  128.4 20.6 %collective-permute-done.5 = bf16[256,2048]{0,1:T(8,128)(2,1)S(1)} collective-permute-done((bf16[256,2048]{0,1:T(8,128)(2,1)S(1)}, bf16[256,2048]{0,1:T(8,128)(2,1)S(1)}, u32[]{:S(2)}, u32[]{:S(2)}) %collective-permute-start.5) | collective-permute-done | bytes 1048608 | tf_op jit(solution)/shard_map/ppermute | solution.py:14
  149.0 22.1 %collective-permute-done.3 = bf16[2048,256]{1,0:T(8,128)(2,1)S(1)} collective-permute-done((bf16[2048,256]{1,0:T(8,128)(2,1)S(1)}, bf16[2048,256]{1,0:T(8,128)(2,1)S(1)}, u32[]{:S(2)}, u32[]{:S(2)}) %collective-permute-start.3) | collective-permute-done | bytes 1048608 | tf_op jit(solution)/shard_map/ppermute | solution.py:14
  174.0 10.3 %fusion.82 = bf16[2048,256]{1,0:T(8,128)(2,1)} fusion(bf16[1,2048,4096]{2,1,0:T(8,128)(2,1)} %param.6, bf16[2048,256]{1,0:T(8,128)(2,1)S(1)} %get-tuple-element.32, bf16[2048,256]{1,0:T(8,128)(2,1)S(1)} %get-tuple-element.31), kind=kOutput, calls=%fused_computation.56 | convolution fusion | flops 4299685888 | bytes 19922944 | tf_op jit(solution)/shard_map/dot_general | solution.py:32
  192.0 10.2 %fusion.76 = bf16[2048,256]{1,0:T(8,128)(2,1)} fusion(bf16[1,2048,4096]{2,1,0:T(8,128)(2,1)} %param.6, bf16[2048,256]{1,0:T(8,128)(2,1)S(1)} %get-tuple-element.34, bf16[2048,256]{1,0:T(8,128)(2,1)S(1)} %get-tuple-element.33), kind=kOutput, calls=%fused_computation.54 | convolution fusion | flops 4299685888 | bytes 19922944 | tf_op jit(solution)/shard_map/dot_general | solution.py:32
  210.2 15.2 %collective-permute-done.7 = bf16[128,2048]{1,0:T(8,128)(2,1)S(1)} collective-permute-done((bf16[128,2048]{1,0:T(8,128)(2,1)S(1)}, bf16[128,2048]{1,0:T(8,128)(2,1)S(1)}, u32[]{:S(2)}, u32[]{:S(2)}) %collective-permute-start.7) | collective-permute-done | bytes 524320 | tf_op jit(solution)/shard_map/ppermute | solution.py:69
  226.2 13.4 %collective-permute-done.8 = bf16[64,2048]{1,0:T(8,128)(2,1)S(1)} collective-permute-done((bf16[64,2048]{1,0:T(8,128)(2,1)S(1)}, bf16[64,2048]{1,0:T(8,128)(2,1)S(1)}, u32[]{:S(2)}, u32[]{:S(2)}) %collective-permute-start.8) | collective-permute-done | bytes 262176 | tf_op jit(solution)/shard_map/ppermute | solution.py:69
  241.8 8.9 %collective-permute-done.9 = bf16[64,2048]{1,0:T(8,128)(2,1)} collective-permute-done((bf16[64,2048]{1,0:T(8,128)(2,1)S(1)}, bf16[64,2048]{1,0:T(8,128)(2,1)}, u32[]{:S(2)}, u32[]{:S(2)}) %collective-permute-start.9) | collective-permute-done | bytes 262176 | tf_op jit(solution)/shard_map/ppermute | solution.py:131
  252.9 11.9 %collective-permute-done.10 = bf16[64,2048]{1,0:T(8,128)(2,1)S(1)} collective-permute-done((bf16[64,2048]{1,0:T(8,128)(2,1)S(1)}, bf16[64,2048]{1,0:T(8,128)(2,1)S(1)}, u32[]{:S(2)}, u32[]{:S(2)}) %collective-permute-start.10) | collective-permute-done | bytes 262176 | tf_op jit(solution)/shard_map/ppermute | solution.py:69
  267.2 11.5 %collective-permute-done.11 = bf16[128,2048]{1,0:T(8,128)(2,1)S(1)} collective-permute-done((bf16[128,2048]{1,0:T(8,128)(2,1)S(1)}, bf16[128,2048]{1,0:T(8,128)(2,1)S(1)}, u32[]{:S(2)}, u32[]{:S(2)}) %collective-permute-start.11) | collective-permute-done | bytes 524320 | tf_op jit(solution)/shard_map/ppermute | solution.py:69
  281.5 11.4 %collective-permute-done.27 = bf16[64,2048]{1,0:T(8,128)(2,1)S(1)} collective-permute-done((bf16[64,2048]{1,0:T(8,128)(2,1)S(1)}, bf16[64,2048]{1,0:T(8,128)(2,1)S(1)}, u32[]{:S(2)}, u32[]{:S(2)}) %collective-permute-start.27) | collective-permute-done | bytes 262176 | tf_op jit(solution)/shard_map/ppermute | solution.py:69
  320.0 21.8 %collective-permute-done.13 = bf16[2048,256]{1,0:T(8,128)(2,1)S(1)} collective-permute-done((bf16[2048,256]{1,0:T(8,128)(2,1)S(1)}, bf16[2048,256]{1,0:T(8,128)(2,1)S(1)}, u32[]{:S(2)}, u32[]{:S(2)}) %collective-permute-start.13) | collective-permute-done | bytes 1048608 | tf_op jit(solution)/shard_map/ppermute | solution.py:14
  343.7 20.2 %collective-permute-done.30 = bf16[2048,256]{1,0:T(8,128)(2,1)S(1)} collective-permute-done((bf16[2048,256]{1,0:T(8,128)(2,1)S(1)}, bf16[2048,256]{1,0:T(8,128)(2,1)S(1)}, u32[]{:S(2)}, u32[]{:S(2)}) %collective-permute-start.30) | collective-permute-done | bytes 1048608 | tf_op jit(solution)/shard_map/ppermute | solution.py:14
  367.2 10.5 %fusion.79 = bf16[2048,256]{1,0:T(8,128)(2,1)} fusion(bf16[1,2048,4096]{2,1,0:T(8,128)(2,1)} %param.6, bf16[2048,256]{1,0:T(8,128)(2,1)S(1)} %get-tuple-element.28, bf16[2048,256]{1,0:T(8,128)(2,1)S(1)} %get-tuple-element.27), kind=kOutput, calls=%fused_computation.55 | convolution fusion | flops 4299685888 | bytes 19922944 | tf_op jit(solution)/shard_map/dot_general | solution.py:32
  379.7 16.8 %convert_bitcast_fusion = bf16[1,4096,2048]{2,1,0:T(8,128)(2,1)} fusion(bf16[512,2048]{1,0:T(8,128)(2,1)} %copy-done.19, bf16[256,2048]{0,1:T(8,128)(2,1)} %get-tuple-element.26, bf16[256,2048]{0,1:T(8,128)(2,1)S(1)} %copy-done.12, bf16[256,2048]{0,1:T(8,128)(2,1)} %get-tuple-element.24, bf16[256,2048]{0,1:T(8,128)(2,1)} %get-tuple-element.23), kind=kOutput, calls=%fused_computation.20 | convolution fusion | flops 8615100416 | bytes 23068672 | tf_op jit(solution)/shard_map/dot_general | solution.py:32
  402.6 10.3 %fusion.85 = bf16[2048,256]{1,0:T(8,128)(2,1)} fusion(bf16[1,2048,4096]{2,1,0:T(8,128)(2,1)} %param.6, bf16[2048,256]{1,0:T(8,128)(2,1)S(1)} %get-tuple-element.30, bf16[2048,256]{1,0:T(8,128)(2,1)S(1)} %get-tuple-element.29), kind=kOutput, calls=%fused_computation.57 | convolution fusion | flops 4299685888 | bytes 19922944 | tf_op jit(solution)/shard_map/dot_general | solution.py:32
  415.6 14.7 %convert_bitcast_fusion.1 = bf16[1,2048,4096]{2,1,0:T(8,128)(2,1)} fusion(bf16[512,2048]{1,0:T(8,128)(2,1)} %copy-done.20, bf16[2048,256]{1,0:T(8,128)(2,1)} %copy-done.17, bf16[2048,256]{1,0:T(8,128)(2,1)} %copy-done.16, bf16[2048,256]{1,0:T(8,128)(2,1)} %copy-done.15, bf16[2048,256]{1,0:T(8,128)(2,1)S(1)} %copy-done.14), kind=kOutput, calls=%fused_computation.21 | convolution fusion | flops 8615100416 | bytes 23068672 | tf_op jit(solution)/shard_map/dot_general | solution.py:32
  434.6 11.5 %collective-permute-done.33 = bf16[64,2048]{1,0:T(8,128)(2,1)S(1)} collective-permute-done((bf16[64,2048]{1,0:T(8,128)(2,1)S(1)}, bf16[64,2048]{1,0:T(8,128)(2,1)S(1)}, u32[]{:S(2)}, u32[]{:S(2)}) %collective-permute-start.33) | collective-permute-done | bytes 262176 | tf_op jit(solution)/shard_map/ppermute | solution.py:69
  (165 shorter events, 105.5 us)
Async XLA Ops:
  2.6 35.7 %collective-permute-start.17 = (bf16[64,2048]{1,0:T(8,128)(2,1)}, bf16[64,2048]{1,0:T(8,128)(2,1)}, u32[]{:S(2)}, u32[]{:S(2)}) collective-permute-start(bf16[64,2048]{1,0:T(8,128)(2,1)} %get-tuple-element.37), channel_id=1, source_target_pairs={{0,8},{4,12},{8,0},{12,4},{1,9},{5,13},{9,1},{13,5},{2,10},{6,14},... | collective-permute-start | bytes 786440 | tf_op jit(solution)/shard_map/ppermute | solution.py:69
  6.6 35.3 %collective-permute-start = (bf16[64,2048]{1,0:T(8,128)(2,1)S(1)}, bf16[64,2048]{1,0:T(8,128)(2,1)}, u32[]{:S(2)}, u32[]{:S(2)}) collective-permute-start(bf16[64,2048]{1,0:T(8,128)(2,1)S(1)} %get-tuple-element.38), channel_id=1, source_target_pairs={{0,8},{4,12},{8,0},{12,4},{1,9},{5,13},{9,1},{13,5},{2,10},{6,14},... | collective-permute-start | bytes 786440 | tf_op jit(solution)/shard_map/ppermute | solution.py:69
  24.9 51.8 %collective-permute-start.21 = (bf16[256,2048]{0,1:T(8,128)(2,1)}, bf16[256,2048]{0,1:T(8,128)(2,1)S(1)}, u32[]{:S(2)}, u32[]{:S(2)}) collective-permute-start(bf16[256,2048]{0,1:T(8,128)(2,1)} %broadcast_select_fusion.4), channel_id=1, source_target_pairs={{0,1},{1,0},{2,3},{3,2},{4,5},{5,4},{6,7},{7,6},{8,9},{9,8},{10,11... | collective-permute-start | bytes 3145736 | tf_op jit(solution)/shard_map/ppermute | solution.py:19
  39.8 14.8 %collective-permute-start.18 = (bf16[128,2048]{1,0:T(8,128)(2,1)S(1)}, bf16[128,2048]{1,0:T(8,128)(2,1)S(1)}, u32[]{:S(2)}, u32[]{:S(2)}) collective-permute-start(bf16[128,2048]{1,0:T(8,128)(2,1)S(1)} %pad_maximum_fusion.2), channel_id=1, source_target_pairs={{0,4},{4,0},{8,12},{12,8},{1,5},{5,1},{9,13},{13,9},{2,6},{6,2},{1... | collective-permute-start | bytes 1572872 | tf_op jit(solution)/shard_map/ppermute | solution.py:69
  41.8 38.8 %collective-permute-start.4 = (bf16[256,2048]{0,1:T(8,128)(2,1)S(1)}, bf16[256,2048]{0,1:T(8,128)(2,1)S(1)}, u32[]{:S(2)}, u32[]{:S(2)}) collective-permute-start(bf16[256,2048]{0,1:T(8,128)(2,1)S(1)} %broadcast_select_fusion.5), channel_id=1, source_target_pairs={{0,1},{1,0},{2,3},{3,2},{4,5},{5,4},{6,7},{7,6},{8,9},{9,8},{10,11... | collective-permute-start | bytes 3145736 | tf_op jit(solution)/shard_map/ppermute | solution.py:19
  42.9 22.8 %collective-permute-start.1 = (bf16[128,2048]{1,0:T(8,128)(2,1)S(1)}, bf16[128,2048]{1,0:T(8,128)(2,1)S(1)}, u32[]{:S(2)}, u32[]{:S(2)}) collective-permute-start(bf16[128,2048]{1,0:T(8,128)(2,1)S(1)} %pad_maximum_fusion), channel_id=1, source_target_pairs={{0,4},{4,0},{8,12},{12,8},{1,5},{5,1},{9,13},{13,9},{2,6},{6,2},{1... | collective-permute-start | bytes 1572872 | tf_op jit(solution)/shard_map/ppermute | solution.py:69
  78.0 26.0 %collective-permute-start.22 = (bf16[256,2048]{0,1:T(8,128)(2,1)S(1)}, bf16[256,2048]{0,1:T(8,128)(2,1)S(1)}, u32[]{:S(2)}, u32[]{:S(2)}) collective-permute-start(bf16[256,2048]{0,1:T(8,128)(2,1)S(1)} %add_convert_fusion.1), channel_id=1, source_target_pairs={{0,2},{1,3},{2,0},{3,1},{4,6},{5,7},{6,4},{7,5},{8,10},{9,11},{10,... | collective-permute-start | bytes 3145736 | tf_op jit(solution)/shard_map/ppermute | solution.py:14
  80.3 46.2 %collective-permute-start.20 = (bf16[2048,256]{1,0:T(8,128)(2,1)S(1)}, bf16[2048,256]{1,0:T(8,128)(2,1)S(1)}, u32[]{:S(2)}, u32[]{:S(2)}) collective-permute-start(bf16[2048,256]{1,0:T(8,128)(2,1)S(1)} %add_convert_fusion.2), channel_id=1, source_target_pairs={{0,2},{1,3},{2,0},{3,1},{4,6},{5,7},{6,4},{7,5},{8,10},{9,11},{10,... | collective-permute-start | bytes 3145736 | tf_op jit(solution)/shard_map/ppermute | solution.py:14
  81.1 67.9 %collective-permute-start.5 = (bf16[256,2048]{0,1:T(8,128)(2,1)S(1)}, bf16[256,2048]{0,1:T(8,128)(2,1)S(1)}, u32[]{:S(2)}, u32[]{:S(2)}) collective-permute-start(bf16[256,2048]{0,1:T(8,128)(2,1)S(1)} %add_convert_fusion.4), channel_id=1, source_target_pairs={{0,2},{1,3},{2,0},{3,1},{4,6},{5,7},{6,4},{7,5},{8,10},{9,11},{10,... | collective-permute-start | bytes 3145736 | tf_op jit(solution)/shard_map/ppermute | solution.py:14
  83.3 87.8 %collective-permute-start.3 = (bf16[2048,256]{1,0:T(8,128)(2,1)S(1)}, bf16[2048,256]{1,0:T(8,128)(2,1)S(1)}, u32[]{:S(2)}, u32[]{:S(2)}) collective-permute-start(bf16[2048,256]{1,0:T(8,128)(2,1)S(1)} %add_convert_fusion.5), channel_id=1, source_target_pairs={{0,2},{1,3},{2,0},{3,1},{4,6},{5,7},{6,4},{7,5},{8,10},{9,11},{10,... | collective-permute-start | bytes 3145736 | tf_op jit(solution)/shard_map/ppermute | solution.py:14
  128.3 45.6 %collective-permute-start.23 = (bf16[2048,256]{1,0:T(8,128)(2,1)S(1)}, bf16[2048,256]{1,0:T(8,128)(2,1)S(1)}, u32[]{:S(2)}, u32[]{:S(2)}) collective-permute-start(bf16[2048,256]{1,0:T(8,128)(2,1)S(1)} %multiply_convert_fusion.3), channel_id=1, source_target_pairs={{0,1},{1,0},{2,3},{3,2},{4,5},{5,4},{6,7},{7,6},{8,9},{9,8},{10,11... | collective-permute-start | bytes 3145736 | tf_op jit(solution)/shard_map/ppermute | solution.py:19
  173.9 16.5 %collective-permute-start.6 = (bf16[2048,256]{1,0:T(8,128)(2,1)}, bf16[2048,256]{1,0:T(8,128)(2,1)}, u32[]{:S(2)}, u32[]{:S(2)}) collective-permute-start(bf16[2048,256]{1,0:T(8,128)(2,1)} %multiply_convert_fusion.5), channel_id=1, source_target_pairs={{0,1},{1,0},{2,3},{3,2},{4,5},{5,4},{6,7},{7,6},{8,9},{9,8},{10,11... | collective-permute-start | bytes 3145736 | tf_op jit(solution)/shard_map/ppermute | solution.py:19
  188.5 17.4 %collective-permute-start.24 = (bf16[128,2048]{1,0:T(8,128)(2,1)}, bf16[128,2048]{1,0:T(8,128)(2,1)}, u32[]{:S(2)}, u32[]{:S(2)}) collective-permute-start(bf16[128,2048]{1,0:T(8,128)(2,1)} %split.131), channel_id=1, source_target_pairs={{0,4},{4,0},{8,12},{12,8},{1,5},{5,1},{9,13},{13,9},{2,6},{6,2},{1... | collective-permute-start | bytes 1572872 | tf_op jit(solution)/shard_map/ppermute | solution.py:69
  205.6 19.7 %collective-permute-start.7 = (bf16[128,2048]{1,0:T(8,128)(2,1)S(1)}, bf16[128,2048]{1,0:T(8,128)(2,1)S(1)}, u32[]{:S(2)}, u32[]{:S(2)}) collective-permute-start(bf16[128,2048]{1,0:T(8,128)(2,1)S(1)} %split.117), channel_id=1, source_target_pairs={{0,4},{4,0},{8,12},{12,8},{1,5},{5,1},{9,13},{13,9},{2,6},{6,2},{1... | collective-permute-start | bytes 1572872 | tf_op jit(solution)/shard_map/ppermute | solution.py:69
  207.3 18.9 %collective-permute-start.25 = (bf16[64,2048]{1,0:T(8,128)(2,1)S(1)}, bf16[64,2048]{1,0:T(8,128)(2,1)S(1)}, u32[]{:S(2)}, u32[]{:S(2)}) collective-permute-start(bf16[64,2048]{1,0:T(8,128)(2,1)S(1)} %split.133), channel_id=1, source_target_pairs={{0,8},{4,12},{8,0},{12,4},{1,9},{5,13},{9,1},{13,5},{2,10},{6,14},... | collective-permute-start | bytes 786440 | tf_op jit(solution)/shard_map/ppermute | solution.py:69
  252.8 27.2 %collective-permute-start.35 = (bf16[256,2048]{0,1:T(8,128)(2,1)S(1)}, bf16[256,2048]{0,1:T(8,128)(2,1)S(1)}, u32[]{:S(2)}, u32[]{:S(2)}) collective-permute-start(bf16[256,2048]{0,1:T(8,128)(2,1)S(1)} %multiply_convert_fusion), channel_id=1, source_target_pairs={{0,1},{1,0},{2,3},{3,2},{4,5},{5,4},{6,7},{7,6},{8,9},{9,8},{10,11... | collective-permute-start | bytes 3145736 | tf_op jit(solution)/shard_map/ppermute | solution.py:19
  265.8 51.5 %collective-permute-start.34 = (bf16[256,2048]{0,1:T(8,128)(2,1)S(1)}, bf16[256,2048]{0,1:T(8,128)(2,1)S(1)}, u32[]{:S(2)}, u32[]{:S(2)}) collective-permute-start(bf16[256,2048]{0,1:T(8,128)(2,1)S(1)} %multiply_convert_fusion.1), channel_id=1, source_target_pairs={{0,1},{1,0},{2,3},{3,2},{4,5},{5,4},{6,7},{7,6},{8,9},{9,8},{10,11... | collective-permute-start | bytes 3145736 | tf_op jit(solution)/shard_map/ppermute | solution.py:19
  315.8 26.0 %collective-permute-start.13 = (bf16[2048,256]{1,0:T(8,128)(2,1)S(1)}, bf16[2048,256]{1,0:T(8,128)(2,1)S(1)}, u32[]{:S(2)}, u32[]{:S(2)}) collective-permute-start(bf16[2048,256]{1,0:T(8,128)(2,1)S(1)} %add_convert_fusion.3), channel_id=1, source_target_pairs={{0,2},{1,3},{2,0},{3,1},{4,6},{5,7},{6,4},{7,5},{8,10},{9,11},{10,... | collective-permute-start | bytes 3145736 | tf_op jit(solution)/shard_map/ppermute | solution.py:14
  319.2 44.6 %collective-permute-start.30 = (bf16[2048,256]{1,0:T(8,128)(2,1)S(1)}, bf16[2048,256]{1,0:T(8,128)(2,1)S(1)}, u32[]{:S(2)}, u32[]{:S(2)}) collective-permute-start(bf16[2048,256]{1,0:T(8,128)(2,1)S(1)} %add_convert_fusion), channel_id=1, source_target_pairs={{0,2},{1,3},{2,0},{3,1},{4,6},{5,7},{6,4},{7,5},{8,10},{9,11},{10,... | collective-permute-start | bytes 3145736 | tf_op jit(solution)/shard_map/ppermute | solution.py:14
  343.5 22.2 %collective-permute-start.14 = (bf16[2048,256]{1,0:T(8,128)(2,1)S(1)}, bf16[2048,256]{1,0:T(8,128)(2,1)S(1)}, u32[]{:S(2)}, u32[]{:S(2)}) collective-permute-start(bf16[2048,256]{1,0:T(8,128)(2,1)S(1)} %multiply_convert_fusion.4), channel_id=1, source_target_pairs={{0,1},{1,0},{2,3},{3,2},{4,5},{5,4},{6,7},{7,6},{8,9},{9,8},{10,11... | collective-permute-start | bytes 3145736 | tf_op jit(solution)/shard_map/ppermute | solution.py:19
  365.6 34.3 %collective-permute-start.31 = (bf16[2048,256]{1,0:T(8,128)(2,1)S(1)}, bf16[2048,256]{1,0:T(8,128)(2,1)}, u32[]{:S(2)}, u32[]{:S(2)}) collective-permute-start(bf16[2048,256]{1,0:T(8,128)(2,1)S(1)} %multiply_convert_fusion.2), channel_id=1, source_target_pairs={{0,1},{1,0},{2,3},{3,2},{4,5},{5,4},{6,7},{7,6},{8,9},{9,8},{10,11... | collective-permute-start | bytes 3145736 | tf_op jit(solution)/shard_map/ppermute | solution.py:19
  379.3 17.2 %collective-permute-start.15 = (bf16[128,2048]{1,0:T(8,128)(2,1)S(1)}, bf16[128,2048]{1,0:T(8,128)(2,1)S(1)}, u32[]{:S(2)}, u32[]{:S(2)}) collective-permute-start(bf16[128,2048]{1,0:T(8,128)(2,1)S(1)} %split.123), channel_id=1, source_target_pairs={{0,4},{4,0},{8,12},{12,8},{1,5},{5,1},{9,13},{13,9},{2,6},{6,2},{1... | collective-permute-start | bytes 1572872 | tf_op jit(solution)/shard_map/ppermute | solution.py:69
  397.4 36.1 %collective-permute-start.16 = (bf16[64,2048]{1,0:T(8,128)(2,1)}, bf16[64,2048]{1,0:T(8,128)(2,1)}, u32[]{:S(2)}, u32[]{:S(2)}) collective-permute-start(bf16[64,2048]{1,0:T(8,128)(2,1)} %split.125), channel_id=1, source_target_pairs={{0,8},{4,12},{8,0},{12,4},{1,9},{5,13},{9,1},{13,5},{2,10},{6,14},... | collective-permute-start | bytes 786440 | tf_op jit(solution)/shard_map/ppermute | solution.py:69
  415.3 15.0 %collective-permute-start.32 = (bf16[128,2048]{1,0:T(8,128)(2,1)}, bf16[128,2048]{1,0:T(8,128)(2,1)}, u32[]{:S(2)}, u32[]{:S(2)}) collective-permute-start(bf16[128,2048]{1,0:T(8,128)(2,1)} %split.137), channel_id=1, source_target_pairs={{0,4},{4,0},{8,12},{12,8},{1,5},{5,1},{9,13},{13,9},{2,6},{6,2},{1... | collective-permute-start | bytes 1572872 | tf_op jit(solution)/shard_map/ppermute | solution.py:69
  (33 other events, 359.4 us)

commit v3 on v2

--- a/solution.py
+++ b/solution.py
@@ -1,7 +1,8 @@
 import jax
 import jax.numpy as jnp
 from jax import lax
-from jax.experimental.layout import Layout, with_layout_constraint
+from jax.experimental import pallas as pl
+from jax.experimental.pallas import tpu as pltpu
 from jax.sharding import PartitionSpec as P
 
 gelu_scale = 0.7978845608028654
@@ -34,19 +35,58 @@
     )
 
 
-def row_major(block):
-    return with_layout_constraint(block, Layout(major_to_minor=(0, 1)))
+def product_kernel(first_ref, second_ref, out_ref):
+    out_ref[...] = jnp.dot(
+        first_ref[...], second_ref[...], preferred_element_type=jnp.float32
+    ).astype(out_ref.dtype)
+
+
+def product(first_op, second_op, stream_first):
+    rows, depth = first_op.shape
+    columns = second_op.shape[1]
+    if stream_first:
+        block = min(512, rows)
+        grid = (rows // block,)
+        in_specs = [
+            pl.BlockSpec((block, depth), lambda i: (i, 0)),
+            pl.BlockSpec((depth, columns), lambda i: (0, 0)),
+        ]
+        out_spec = pl.BlockSpec((block, columns), lambda i: (i, 0))
+    else:
+        block = min(512, columns)
+        grid = (columns // block,)
+        in_specs = [
+            pl.BlockSpec((rows, depth), lambda i: (0, 0)),
+            pl.BlockSpec((depth, block), lambda i: (0, i)),
+        ]
+        out_spec = pl.BlockSpec((rows, block), lambda i: (0, i))
+    return pl.pallas_call(
+        product_kernel,
+        grid=grid,
+        in_specs=in_specs,
+        out_specs=out_spec,
+        out_shape=jax.ShapeDtypeStruct((rows, columns), jnp.bfloat16),
+        compiler_params=pltpu.CompilerParams(vmem_limit_bytes=28 * 2**20),
+        cost_estimate=pl.CostEstimate(
+            flops=2 * rows * depth * columns,
+            bytes_accessed=2 * (rows * depth + depth * columns + rows * columns),
+            transcendentals=0,
+        ),
+    )(first_op, second_op)
 
 
 def turned(block):
-    return row_major(block.T)
-
-
-def sum_half(part, axis, is_odd):
+    return lax.optimization_barrier(block.T)
+
+
+def chip_half(part, axis, is_odd):
     low, high = jnp.split(part, 2, axis=axis)
     got = from_partner(jnp.where(is_odd, low, high))
     mine = jnp.where(is_odd, high, low)
-    chip = (mine.astype(jnp.float32) + got.astype(jnp.float32)).astype(jnp.bfloat16)
+    return (mine.astype(jnp.float32) + got.astype(jnp.float32)).astype(jnp.bfloat16)
+
+
+def sum_chips(chip):
     total = chip.astype(jnp.float32)
     for step in range(1, lax.axis_size("narrow") // 2):
         total = total + shifted(chip, "narrow", 2 * step).astype(jnp.float32)
@@ -113,32 +153,41 @@
     ]
     own = [upstream[c * rows : (c + 1) * rows] for c in range(chunks)]
 
-    def backward(incoming, own_rows, slopes):
-        part = row_major(contract(w_down, turned(incoming), (1, 0)).astype(jnp.bfloat16))
-        back = sum_half(part, 0, is_odd)
-        slope = row_major(both_halves((back * slopes).astype(jnp.bfloat16), 0, is_odd))
-        part = row_major(contract(w_up, slope, (1, 0)).astype(jnp.bfloat16))
+    def back_chip(incoming):
+        return chip_half(product(w_down, turned(incoming), True), 0, is_odd)
+
+    def onward(back, own_rows, slopes):
+        slope = both_halves((back * slopes).astype(jnp.bfloat16), 0, is_odd)
+        part = product(w_up, slope, True)
         return slope, scatter_wide(turned(part), own_rows)
 
+    first_in = [gather_wide(own[c]) for c in range(chunks)]
+    chips = [chip_half(product(saved[c], w_up, False), 1, is_odd) for c in range(chunks)]
     hidden, slopes, second = [], [], []
     for c in range(chunks):
-        first_in = gather_wide(own[c])
-        part = contract(saved[c], w_up, (1, 0)).astype(jnp.bfloat16)
-        act, slope_of = gelu_parts(sum_half(part, 1, is_odd))
-        hidden.append(both_halves(act.astype(jnp.bfloat16), 1, is_odd))
-        slopes.append(turned(slope_of))
-        _, grad = backward(first_in, own[c], slopes[c])
+        act, slope_of = gelu_parts(sum_chips(chips[c]))
+        hidden.append(act.astype(jnp.bfloat16))
+        slope_of, first_in[c] = lax.optimization_barrier((slope_of.T, first_in[c]))
+        slopes.append(slope_of)
+    chips = [back_chip(first_in[c]) for c in range(chunks)]
+    for c in range(chunks):
+        _, grad = onward(sum_chips(chips[c]), own[c], slopes[c])
         second.append(lax.ppermute(grad, "section", [(1, 0)]))
-    incoming, slope, grads = [], [], []
+    hidden = [both_halves(one, 1, is_odd) for one in hidden]
+    own = [jnp.where(is_upper, own[c], second[c]) for c in range(chunks)]
+    incoming = [gather_wide(own[c]) for c in range(chunks)]
+    chips = [back_chip(incoming[c]) for c in range(chunks)]
+    back = [sum_chips(one) for one in chips]
+    all_hidden, _ = lax.optimization_barrier((jnp.concatenate(hidden, axis=0), chips[-1]))
+    grad_down = contract(all_hidden, jnp.concatenate(incoming, axis=0), (0, 0)).astype(
+        jnp.bfloat16
+    )
+    grad_down, back[0] = lax.optimization_barrier((grad_down, back[0]))
+    slope, grads = [], []
     for c in range(chunks):
-        own_rows = jnp.where(is_upper, own[c], second[c])
-        incoming.append(gather_wide(own_rows))
-        one_slope, grad = backward(incoming[c], own_rows, slopes[c])
+        one_slope, grad = onward(back[c], own[c], slopes[c])
         slope.append(one_slope)
         grads.append(grad)
-    grad_down = contract(
-        jnp.concatenate(hidden, axis=0), jnp.concatenate(incoming, axis=0), (0, 0)
-    ).astype(jnp.bfloat16)
     grad_up = contract(
         jnp.concatenate(saved, axis=0), jnp.concatenate(slope, axis=1), (0, 1)
     ).astype(jnp.bfloat16)

time: 451 us -> 485 us (1.075); the launches traced: 447 us -> 476 us
  matrix products: 134 us -> 30.8 us
  Pallas kernels: 0 us -> 57.9 us
  other arithmetic: 30 us -> 57.5 us
  local copies, waits for them, and re-layouts: 24.9 us -> 51.8 us
  waiting for transfers between devices: 228 us -> 245 us
    dot_general x12 -> x2, matrix products: 134 us -> 30.8 us  [contract(): lax.dot_general(first_op, second_op, ((dims[:1], dims[1:]), ((), ())), pr...]
    ppermute x16, waiting for transfers between devices: 91.4 us -> 155 us  [from_place(): lax.ppermute(block, 'wide', [(i, i ^ mask) for i in range(lax.axis_size('...]
    pallas_call x0 -> x10, Pallas kernels: none -> 57.9 us  [product(): pl.pallas_call(product_kernel, grid=grid, in_specs=in_specs, out_specs=ou...]
    ppermute x6, waiting for transfers between devices: 128 us -> 76.1 us  [shifted(): lax.ppermute(block, axis, [(i, (i + distance) % size) for i in range(size)])]
    unnamed x52 -> x106, local copies, waits for them, and re-layouts: 10.5 us -> 40.1 us
    concatenate x0 -> x7, other arithmetic: none -> 16.6 us  [the longest x1 15.9 us: body(): jnp.concatenate(hidden, axis=0)]
    another operation x4 -> x0, local copies, waits for them, and re-layouts: 7.67 us -> none  [row_major(): return with_layout_constraint(block, Layout(major_to_minor=(0, 1)))]
    convert_element_type x12 -> x11, other arithmetic: 12 us -> 17.8 us  [the longest x6 9.1 us: chip_half(): (mine.astype(jnp.float32) + got.astype(jnp.float32)).astype(jnp.bfloat16)]
  transfers between devices with their start and end apart: 36 -> 36, of which waited for: 15 -> 22; matrix products, arithmetic and copies ran while one was open for 40% -> 22% of each run, Pallas kernels for 0% -> 12%
where the time goes in v3:
time: 485 us; the launch traced here: 476 us
  waiting for transfers between devices  245 us (51%)
  Pallas kernels  57.9 us (12%)
  other arithmetic  57.5 us (12%)
  local copies, waits for them, and re-layouts  51.8 us (11%)
  starting transfers between devices  31.2 us (6%)
  matrix products  30.8 us (6%)
    ppermute x16, waiting for transfers between devices, from_place(): lax.ppermute(block, 'wide', [(i, i ^ mask) for i in range(lax.axis_size('...  155 us
    ppermute x6, waiting for transfers between devices, shifted(): lax.ppermute(block, axis, [(i, (i + distance) % size) for i in range(size)])  76.1 us
    pallas_call x10, Pallas kernels, product(): pl.pallas_call(product_kernel, grid=grid, in_specs=in_specs, out_specs=ou...  57.9 us
    unnamed x106, local copies, waits for them, and re-layouts  40.1 us
    dot_general x2, matrix products, contract(): lax.dot_general(first_op, second_op, ((dims[:1], dims[1:]), ((), ())), pr...  30.8 us
    ppermute x16, starting transfers between devices, from_place(): lax.ppermute(block, 'wide', [(i, i ^ mask) for i in range(lax.axis_size('...  17.9 us
    concatenate x1, other arithmetic, body(): jnp.concatenate(hidden, axis=0)  15.9 us
    ppermute x2, waiting for transfers between devices, body(): second.append(lax.ppermute(grad, 'section', [(1, 0)]))  13 us
  transfers between devices with their start and end apart: 36, of which 22 were waited for; matrix products, arithmetic and copies ran while one was open for 22% of the time, Pallas kernels for 12%

profile of v3, /device:TPU:0, one launch (start us, length us, event | category | flops | bytes accessed | tf_op | source)
XLA Modules:
  0.0 476.0 jit_solution(17053252896386069167)
XLA Ops:
  16.3 7.1 %shard_map.70 = bf16[256,4096]{1,0:T(8,128)(2,1)S(1)} custom-call(bf16[256,2048]{1,0:T(8,128)(2,1)S(1)} %pad_maximum_fusion.6.first_ref, bf16[2048,4096]{1,0:T(8,128)(2,1)S(1)} %bitcast.49), custom_call_target="tpu_custom_call" | custom-call | flops 4294967296 | bytes 19922944 | tf_op jit(solution)/shard_map/pallas_call | solution.py:63
  34.1 7.1 %shard_map.67 = bf16[256,4096]{1,0:T(8,128)(2,1)S(1)} custom-call(bf16[256,2048]{1,0:T(8,128)(2,1)S(1)} %pad_maximum_fusion.4.first_ref, bf16[2048,4096]{1,0:T(8,128)(2,1)S(1)} %bitcast.50), custom_call_target="tpu_custom_call" | custom-call | flops 4294967296 | bytes 19922944 | tf_op jit(solution)/shard_map/pallas_call | solution.py:63
  57.2 7.0 %collective-permute-done.15 = bf16[128,2048]{0,1:T(8,128)(2,1)S(1)} collective-permute-done((bf16[128,2048]{0,1:T(8,128)(2,1)S(1)}, bf16[128,2048]{0,1:T(8,128)(2,1)S(1)}, u32[]{:S(2)}, u32[]{:S(2)}) %collective-permute-start.15) | collective-permute-done | bytes 524320 | tf_op jit(solution)/shard_map/ppermute | solution.py:109
  65.8 9.0 %collective-permute-done.3 = bf16[128,2048]{0,1:T(8,128)(2,1)S(1)} collective-permute-done((bf16[128,2048]{0,1:T(8,128)(2,1)S(1)}, bf16[128,2048]{0,1:T(8,128)(2,1)S(1)}, u32[]{:S(2)}, u32[]{:S(2)}) %collective-permute-start.3) | collective-permute-done | bytes 524320 | tf_op jit(solution)/shard_map/ppermute | solution.py:109
  84.3 6.5 %copy-done.3 = bf16[1,4096,2048]{2,1,0:T(8,128)(2,1)S(1)} copy-done((bf16[1,4096,2048]{2,1,0:T(8,128)(2,1)S(1)}, bf16[1,4096,2048]{2,1,0:T(8,128)(2,1)}, u32[]{:S(2)}) %copy-start.3) | copy-done | bytes 16777240
  96.8 6.2 %collective-permute-done.1 = bf16[256,2048]{0,1:T(8,128)(2,1)S(1)} collective-permute-done((bf16[256,2048]{0,1:T(8,128)(2,1)S(1)}, bf16[256,2048]{0,1:T(8,128)(2,1)S(1)}, u32[]{:S(2)}, u32[]{:S(2)}) %collective-permute-start.1) | collective-permute-done | bytes 1048608 | tf_op jit(solution)/shard_map/ppermute | solution.py:15
  105.6 5.9 %shard_map.68 = bf16[4096,256]{1,0:T(8,128)(2,1)S(1)} custom-call(bf16[4096,2048]{1,0:T(8,128)(2,1)S(1)} %bitcast.58, bf16[2048,256]{1,0:T(8,128)(2,1)S(1)} %bitcast.71), custom_call_target="tpu_custom_call" | custom-call | flops 4294967296 | bytes 19922944 | tf_op jit(solution)/shard_map/pallas_call | solution.py:63
  117.3 20.9 %collective-permute-done.17 = bf16[2048,256]{1,0:T(8,128)(2,1)S(1)} collective-permute-done((bf16[2048,256]{1,0:T(8,128)(2,1)S(1)}, bf16[2048,256]{1,0:T(8,128)(2,1)S(1)}, u32[]{:S(2)}, u32[]{:S(2)}) %collective-permute-start.17) | collective-permute-done | bytes 1048608 | tf_op jit(solution)/shard_map/ppermute | solution.py:15
  140.1 20.2 %collective-permute-done.5 = bf16[2048,256]{1,0:T(8,128)(2,1)} collective-permute-done((bf16[2048,256]{1,0:T(8,128)(2,1)}, bf16[2048,256]{1,0:T(8,128)(2,1)}, u32[]{:S(2)}, u32[]{:S(2)}) %collective-permute-start.5) | collective-permute-done | bytes 1048608 | tf_op jit(solution)/shard_map/ppermute | solution.py:15
  193.7 16.7 %collective-permute-done.7 = bf16[128,2048]{0,1:T(8,128)(2,1)S(1)} collective-permute-done((bf16[128,2048]{0,1:T(8,128)(2,1)S(1)}, bf16[128,2048]{0,1:T(8,128)(2,1)S(1)}, u32[]{:S(2)}, u32[]{:S(2)}) %collective-permute-start.7) | collective-permute-done | bytes 524320 | tf_op jit(solution)/shard_map/ppermute | solution.py:109
  210.8 18.2 %collective-permute-done.20 = bf16[64,2048]{0,1:T(8,128)(2,1)S(1)} collective-permute-done((bf16[64,2048]{0,1:T(8,128)(2,1)S(1)}, bf16[64,2048]{0,1:T(8,128)(2,1)S(1)}, u32[]{:S(2)}, u32[]{:S(2)}) %collective-permute-start.20) | collective-permute-done | bytes 262176 | tf_op jit(solution)/shard_map/ppermute | solution.py:109
  230.5 8.3 %collective-permute-done.8 = bf16[64,2048]{0,1:T(8,128)(2,1)S(1)} collective-permute-done((bf16[64,2048]{0,1:T(8,128)(2,1)S(1)}, bf16[64,2048]{0,1:T(8,128)(2,1)S(1)}, u32[]{:S(2)}, u32[]{:S(2)}) %collective-permute-start.8) | collective-permute-done | bytes 262176 | tf_op jit(solution)/shard_map/ppermute | solution.py:109
  242.3 11.4 %collective-permute-done.9 = bf16[64,2048]{0,1:T(8,128)(2,1)S(1)} collective-permute-done((bf16[64,2048]{0,1:T(8,128)(2,1)S(1)}, bf16[64,2048]{0,1:T(8,128)(2,1)S(1)}, u32[]{:S(2)}, u32[]{:S(2)}) %collective-permute-start.9) | collective-permute-done | bytes 262176 | tf_op jit(solution)/shard_map/ppermute | solution.py:175
  253.9 22.3 %collective-permute-done.22 = bf16[64,2048]{0,1:T(8,128)(2,1)S(1)} collective-permute-done((bf16[64,2048]{0,1:T(8,128)(2,1)S(1)}, bf16[64,2048]{0,1:T(8,128)(2,1)S(1)}, u32[]{:S(2)}, u32[]{:S(2)}) %collective-permute-start.22) | collective-permute-done | bytes 262176 | tf_op jit(solution)/shard_map/ppermute | solution.py:109
  278.0 9.5 %collective-permute-done.25 = bf16[64,2048]{0,1:T(8,128)(2,1)S(1)} collective-permute-done((bf16[64,2048]{0,1:T(8,128)(2,1)S(1)}, bf16[64,2048]{0,1:T(8,128)(2,1)S(1)}, u32[]{:S(2)}, u32[]{:S(2)}) %collective-permute-start.25) | collective-permute-done | bytes 262176 | tf_op jit(solution)/shard_map/ppermute | solution.py:109
  287.8 10.8 %collective-permute-done.23 = bf16[128,2048]{0,1:T(8,128)(2,1)S(1)} collective-permute-done((bf16[128,2048]{0,1:T(8,128)(2,1)S(1)}, bf16[128,2048]{0,1:T(8,128)(2,1)S(1)}, u32[]{:S(2)}, u32[]{:S(2)}) %collective-permute-start.23) | collective-permute-done | bytes 524320 | tf_op jit(solution)/shard_map/ppermute | solution.py:109
  299.2 6.1 %shard_map.73 = bf16[4096,256]{1,0:T(8,128)(2,1)S(1)} custom-call(bf16[4096,2048]{1,0:T(8,128)(2,1)S(1)} %bitcast.61, bf16[2048,256]{1,0:T(8,128)(2,1)S(1)} %maximum_bitcast_fusion.second_ref), custom_call_target="tpu_custom_call" | custom-call | flops 4294967296 | bytes 19922944 | tf_op jit(solution)/shard_map/pallas_call | solution.py:63
  317.7 15.9 %maximum_maximum_fusion = bf16[512,4096]{0,1:T(8,128)(2,1)} fusion(bf16[256,2048]{0,1:T(8,128)(2,1)S(1)} %get-tuple-element.47, bf16[256,2048]{0,1:T(8,128)(2,1)S(1)} %get-tuple-element.46, bf16[256,2048]{0,1:T(8,128)(2,1)S(1)} %get-tuple-element.43, bf16[256,2048]{0,1:T(8,128)(2,1)S(1)} %get-tuple-element.42), kind=kLoop, calls=%fused_computation.2 | loop fusion | flops 16777216 | bytes 8388608 | tf_op jit(solution)/shard_map/concatenate | solution.py:181
  346.8 15.4 %convolution_convert_fusion = bf16[4096,2048]{1,0:T(8,128)(2,1)} fusion(bf16[512,4096]{0,1:T(8,128)(2,1)} %maximum_maximum_fusion, bf16[512,2048]{0,1:T(8,128)(2,1)} %concatenate.83), kind=kOutput, calls=%fused_computation.1 | convolution fusion | flops 8598323200 | bytes 23068672 | tf_op jit(solution)/shard_map/dot_general | solution.py:33
  362.2 6.3 %collective-permute-done.32 = bf16[2048,256]{1,0:T(8,128)(2,1)} collective-permute-done((bf16[2048,256]{1,0:T(8,128)(2,1)}, bf16[2048,256]{1,0:T(8,128)(2,1)}, u32[]{:S(2)}, u32[]{:S(2)}) %collective-permute-start.32) | collective-permute-done | bytes 1048608 | tf_op jit(solution)/shard_map/ppermute | solution.py:15
  371.0 19.1 %collective-permute-done.28 = bf16[2048,256]{1,0:T(8,128)(2,1)} collective-permute-done((bf16[2048,256]{1,0:T(8,128)(2,1)}, bf16[2048,256]{1,0:T(8,128)(2,1)}, u32[]{:S(2)}, u32[]{:S(2)}) %collective-permute-start.28) | collective-permute-done | bytes 1048608 | tf_op jit(solution)/shard_map/ppermute | solution.py:15
  408.9 15.4 %convert_bitcast_fusion = bf16[1,2048,4096]{2,1,0:T(8,128)(2,1)} fusion(bf16[512,2048]{1,0:T(8,128)(2,1)} %copy-done.37, bf16[2048,256]{1,0:T(8,128)(2,1)} %copy-done.28, bf16[2048,256]{1,0:T(8,128)(2,1)} %copy-done.27, bf16[2048,256]{1,0:T(8,128)(2,1)} %copy-done.30, bf16[2048,256]{1,0:T(8,128)(2,1)} %copy-done.29), kind=kOutput, calls=%fused_computation | convolution fusion | flops 8615100416 | bytes 23068672 | tf_op jit(solution)/shard_map/dot_general | solution.py:33
  429.2 34.5 %collective-permute-done.35 = bf16[64,2048]{0,1:T(8,128)(2,1)S(1)} collective-permute-done((bf16[64,2048]{0,1:T(8,128)(2,1)S(1)}, bf16[64,2048]{0,1:T(8,128)(2,1)S(1)}, u32[]{:S(2)}, u32[]{:S(2)}) %collective-permute-start.35) | collective-permute-done | bytes 262176 | tf_op jit(solution)/shard_map/ppermute | solution.py:109
  463.9 10.3 %collective-permute-done.31 = bf16[64,2048]{0,1:T(8,128)(2,1)S(1)} collective-permute-done((bf16[64,2048]{0,1:T(8,128)(2,1)S(1)}, bf16[64,2048]{0,1:T(8,128)(2,1)S(1)}, u32[]{:S(2)}, u32[]{:S(2)}) %collective-permute-start.31) | collective-permute-done | bytes 262176 | tf_op jit(solution)/shard_map/ppermute | solution.py:109
  (232 shorter events, 163.9 us)
Async XLA Ops:
  2.1 45.9 %collective-permute-start.14 = (bf16[64,2048]{0,1:T(8,128)(2,1)S(1)}, bf16[64,2048]{0,1:T(8,128)(2,1)}, u32[]{:S(2)}, u32[]{:S(2)}) collective-permute-start(bf16[64,2048]{0,1:T(8,128)(2,1)S(1)} %copy.19), channel_id=1, source_target_pairs={{0,8},{4,12},{8,0},{12,4},{1,9},{5,13},{9,1},{13,5},{2,10},{6,14},... | collective-permute-start | bytes 786440 | tf_op jit(solution)/shard_map/ppermute | solution.py:109
  6.5 45.5 %collective-permute-start.2 = (bf16[64,2048]{0,1:T(8,128)(2,1)S(1)}, bf16[64,2048]{0,1:T(8,128)(2,1)}, u32[]{:S(2)}, u32[]{:S(2)}) collective-permute-start(bf16[64,2048]{0,1:T(8,128)(2,1)S(1)} %copy.14), channel_id=1, source_target_pairs={{0,8},{4,12},{8,0},{12,4},{1,9},{5,13},{9,1},{13,5},{2,10},{6,14},... | collective-permute-start | bytes 786440 | tf_op jit(solution)/shard_map/ppermute | solution.py:109
  27.7 26.3 %collective-permute-start.11 = (bf16[256,2048]{0,1:T(8,128)(2,1)}, bf16[256,2048]{0,1:T(8,128)(2,1)}, u32[]{:S(2)}, u32[]{:S(2)}) collective-permute-start(bf16[256,2048]{0,1:T(8,128)(2,1)} %broadcast_select_fusion.2), channel_id=1, source_target_pairs={{0,1},{1,0},{2,3},{3,2},{4,5},{5,4},{6,7},{7,6},{8,9},{9,8},{10,11... | collective-permute-start | bytes 3145736 | tf_op jit(solution)/shard_map/ppermute | solution.py:20
  46.8 29.4 %collective-permute-start = (bf16[256,2048]{0,1:T(8,128)(2,1)S(1)}, bf16[256,2048]{0,1:T(8,128)(2,1)S(1)}, u32[]{:S(2)}, u32[]{:S(2)}) collective-permute-start(bf16[256,2048]{0,1:T(8,128)(2,1)S(1)} %broadcast_select_fusion.5), channel_id=1, source_target_pairs={{0,1},{1,0},{2,3},{3,2},{4,5},{5,4},{6,7},{7,6},{8,9},{9,8},{10,11... | collective-permute-start | bytes 3145736 | tf_op jit(solution)/shard_map/ppermute | solution.py:20
  55.6 26.1 %collective-permute-start.12 = (bf16[256,2048]{0,1:T(8,128)(2,1)S(1)}, bf16[256,2048]{0,1:T(8,128)(2,1)S(1)}, u32[]{:S(2)}, u32[]{:S(2)}) collective-permute-start(bf16[256,2048]{0,1:T(8,128)(2,1)S(1)} %add_convert_fusion.3), channel_id=1, source_target_pairs={{0,2},{1,3},{2,0},{3,1},{4,6},{5,7},{6,4},{7,5},{8,10},{9,11},{10,... | collective-permute-start | bytes 3145736 | tf_op jit(solution)/shard_map/ppermute | solution.py:15
  76.7 26.3 %collective-permute-start.1 = (bf16[256,2048]{0,1:T(8,128)(2,1)S(1)}, bf16[256,2048]{0,1:T(8,128)(2,1)S(1)}, u32[]{:S(2)}, u32[]{:S(2)}) collective-permute-start(bf16[256,2048]{0,1:T(8,128)(2,1)S(1)} %add_convert_fusion.5), channel_id=1, source_target_pairs={{0,2},{1,3},{2,0},{3,1},{4,6},{5,7},{6,4},{7,5},{8,10},{9,11},{10,... | collective-permute-start | bytes 3145736 | tf_op jit(solution)/shard_map/ppermute | solution.py:15
  112.2 26.0 %collective-permute-start.17 = (bf16[2048,256]{1,0:T(8,128)(2,1)S(1)}, bf16[2048,256]{1,0:T(8,128)(2,1)S(1)}, u32[]{:S(2)}, u32[]{:S(2)}) collective-permute-start(bf16[2048,256]{1,0:T(8,128)(2,1)S(1)} %add_convert_fusion.2), channel_id=1, source_target_pairs={{0,2},{1,3},{2,0},{3,1},{4,6},{5,7},{6,4},{7,5},{8,10},{9,11},{10,... | collective-permute-start | bytes 3145736 | tf_op jit(solution)/shard_map/ppermute | solution.py:15
  115.8 44.6 %collective-permute-start.5 = (bf16[2048,256]{1,0:T(8,128)(2,1)}, bf16[2048,256]{1,0:T(8,128)(2,1)}, u32[]{:S(2)}, u32[]{:S(2)}) collective-permute-start(bf16[2048,256]{1,0:T(8,128)(2,1)} %add_convert_fusion.4), channel_id=1, source_target_pairs={{0,2},{1,3},{2,0},{3,1},{4,6},{5,7},{6,4},{7,5},{8,10},{9,11},{10,... | collective-permute-start | bytes 3145736 | tf_op jit(solution)/shard_map/ppermute | solution.py:15
  139.6 22.7 %collective-permute-start.18 = (bf16[2048,256]{1,0:T(8,128)(2,1)}, bf16[2048,256]{1,0:T(8,128)(2,1)}, u32[]{:S(2)}, u32[]{:S(2)}) collective-permute-start(bf16[2048,256]{1,0:T(8,128)(2,1)} %multiply_convert_fusion.2), channel_id=1, source_target_pairs={{0,1},{1,0},{2,3},{3,2},{4,5},{5,4},{6,7},{7,6},{8,9},{9,8},{10,11... | collective-permute-start | bytes 3145736 | tf_op jit(solution)/shard_map/ppermute | solution.py:20
  139.6 43.0 %collective-permute-start.13 = (bf16[256,2048]{0,1:T(8,128)(2,1)}, bf16[256,2048]{0,1:T(8,128)(2,1)}, u32[]{:S(2)}, u32[]{:S(2)}) collective-permute-start(bf16[256,2048]{0,1:T(8,128)(2,1)} %get-tuple-element.48), channel_id=1, source_target_pairs={{0,1},{1,0},{2,3},{3,2},{4,5},{5,4},{6,7},{7,6},{8,9},{9,8},{10,11... | collective-permute-start | bytes 3145736 | tf_op jit(solution)/shard_map/ppermute | solution.py:20
  140.1 136.5 %collective-permute-start.10 = (bf16[256,2048]{0,1:T(8,128)(2,1)}, bf16[256,2048]{0,1:T(8,128)(2,1)}, u32[]{:S(2)}, u32[]{:S(2)}) collective-permute-start(bf16[256,2048]{0,1:T(8,128)(2,1)} %get-tuple-element.41), channel_id=1, source_target_pairs={{0,1},{1,0},{2,3},{3,2},{4,5},{5,4},{6,7},{7,6},{8,9},{9,8},{10,11... | collective-permute-start | bytes 3145736 | tf_op jit(solution)/shard_map/ppermute | solution.py:20
  181.1 29.2 %collective-permute-start.7 = (bf16[128,2048]{0,1:T(8,128)(2,1)S(1)}, bf16[128,2048]{0,1:T(8,128)(2,1)S(1)}, u32[]{:S(2)}, u32[]{:S(2)}) collective-permute-start(bf16[128,2048]{0,1:T(8,128)(2,1)S(1)} %split.117), channel_id=1, source_target_pairs={{0,4},{4,0},{8,12},{12,8},{1,5},{5,1},{9,13},{13,9},{2,6},{6,2},{1... | collective-permute-start | bytes 1572872 | tf_op jit(solution)/shard_map/ppermute | solution.py:109
  190.1 38.9 %collective-permute-start.20 = (bf16[64,2048]{0,1:T(8,128)(2,1)S(1)}, bf16[64,2048]{0,1:T(8,128)(2,1)S(1)}, u32[]{:S(2)}, u32[]{:S(2)}) collective-permute-start(bf16[64,2048]{0,1:T(8,128)(2,1)S(1)} %split.127), channel_id=1, source_target_pairs={{0,8},{4,12},{8,0},{12,4},{1,9},{5,13},{9,1},{13,5},{2,10},{6,14},... | collective-permute-start | bytes 786440 | tf_op jit(solution)/shard_map/ppermute | solution.py:109
  210.7 28.1 %collective-permute-start.8 = (bf16[64,2048]{0,1:T(8,128)(2,1)S(1)}, bf16[64,2048]{0,1:T(8,128)(2,1)S(1)}, u32[]{:S(2)}, u32[]{:S(2)}) collective-permute-start(bf16[64,2048]{0,1:T(8,128)(2,1)S(1)} %split.119), channel_id=1, source_target_pairs={{0,8},{4,12},{8,0},{12,4},{1,9},{5,13},{9,1},{13,5},{2,10},{6,14},... | collective-permute-start | bytes 786440 | tf_op jit(solution)/shard_map/ppermute | solution.py:109
  242.3 33.9 %collective-permute-start.22 = (bf16[64,2048]{0,1:T(8,128)(2,1)S(1)}, bf16[64,2048]{0,1:T(8,128)(2,1)S(1)}, u32[]{:S(2)}, u32[]{:S(2)}) collective-permute-start(bf16[64,2048]{0,1:T(8,128)(2,1)S(1)} %broadcast_select_fusion.18), channel_id=1, source_target_pairs={{0,8},{4,12},{8,0},{12,4},{1,9},{5,13},{9,1},{13,5},{2,10},{6,14},... | collective-permute-start | bytes 786440 | tf_op jit(solution)/shard_map/ppermute | solution.py:109
  253.8 33.7 %collective-permute-start.25 = (bf16[64,2048]{0,1:T(8,128)(2,1)S(1)}, bf16[64,2048]{0,1:T(8,128)(2,1)S(1)}, u32[]{:S(2)}, u32[]{:S(2)}) collective-permute-start(bf16[64,2048]{0,1:T(8,128)(2,1)S(1)} %broadcast_select_fusion.19), channel_id=1, source_target_pairs={{0,8},{4,12},{8,0},{12,4},{1,9},{5,13},{9,1},{13,5},{2,10},{6,14},... | collective-permute-start | bytes 786440 | tf_op jit(solution)/shard_map/ppermute | solution.py:109
  276.5 22.2 %collective-permute-start.23 = (bf16[128,2048]{0,1:T(8,128)(2,1)S(1)}, bf16[128,2048]{0,1:T(8,128)(2,1)S(1)}, u32[]{:S(2)}, u32[]{:S(2)}) collective-permute-start(bf16[128,2048]{0,1:T(8,128)(2,1)S(1)} %pad_maximum_fusion.10), channel_id=1, source_target_pairs={{0,4},{4,0},{8,12},{12,8},{1,5},{5,1},{9,13},{13,9},{2,6},{6,2},{1... | collective-permute-start | bytes 1572872 | tf_op jit(solution)/shard_map/ppermute | solution.py:109
  307.8 31.6 %collective-permute-start.24 = (bf16[2048,256]{1,0:T(8,128)(2,1)}, bf16[2048,256]{1,0:T(8,128)(2,1)}, u32[]{:S(2)}, u32[]{:S(2)}) collective-permute-start(bf16[2048,256]{1,0:T(8,128)(2,1)} %broadcast_select_fusion.11), channel_id=1, source_target_pairs={{0,1},{1,0},{2,3},{3,2},{4,5},{5,4},{6,7},{7,6},{8,9},{9,8},{10,11... | collective-permute-start | bytes 3145736 | tf_op jit(solution)/shard_map/ppermute | solution.py:20
  317.3 26.3 %collective-permute-start.27 = (bf16[2048,256]{1,0:T(8,128)(2,1)}, bf16[2048,256]{1,0:T(8,128)(2,1)}, u32[]{:S(2)}, u32[]{:S(2)}) collective-permute-start(bf16[2048,256]{1,0:T(8,128)(2,1)} %broadcast_select_fusion.10), channel_id=1, source_target_pairs={{0,1},{1,0},{2,3},{3,2},{4,5},{5,4},{6,7},{7,6},{8,9},{9,8},{10,11... | collective-permute-start | bytes 3145736 | tf_op jit(solution)/shard_map/ppermute | solution.py:20
  342.1 26.3 %collective-permute-start.32 = (bf16[2048,256]{1,0:T(8,128)(2,1)}, bf16[2048,256]{1,0:T(8,128)(2,1)}, u32[]{:S(2)}, u32[]{:S(2)}) collective-permute-start(bf16[2048,256]{1,0:T(8,128)(2,1)} %add_convert_fusion.1), channel_id=1, source_target_pairs={{0,2},{1,3},{2,0},{3,1},{4,6},{5,7},{6,4},{7,5},{8,10},{9,11},{10,... | collective-permute-start | bytes 3145736 | tf_op jit(solution)/shard_map/ppermute | solution.py:15
  346.2 43.9 %collective-permute-start.28 = (bf16[2048,256]{1,0:T(8,128)(2,1)}, bf16[2048,256]{1,0:T(8,128)(2,1)}, u32[]{:S(2)}, u32[]{:S(2)}) collective-permute-start(bf16[2048,256]{1,0:T(8,128)(2,1)} %add_convert_fusion), channel_id=1, source_target_pairs={{0,2},{1,3},{2,0},{3,1},{4,6},{5,7},{6,4},{7,5},{8,10},{9,11},{10,... | collective-permute-start | bytes 3145736 | tf_op jit(solution)/shard_map/ppermute | solution.py:15
  400.0 24.3 %collective-permute-start.34 = (bf16[128,2048]{0,1:T(8,128)(2,1)}, bf16[128,2048]{0,1:T(8,128)(2,1)}, u32[]{:S(2)}, u32[]{:S(2)}) collective-permute-start(bf16[128,2048]{0,1:T(8,128)(2,1)} %split.137), channel_id=1, source_target_pairs={{0,4},{4,0},{8,12},{12,8},{1,5},{5,1},{9,13},{13,9},{2,6},{6,2},{1... | collective-permute-start | bytes 1572872 | tf_op jit(solution)/shard_map/ppermute | solution.py:109
  425.8 37.9 %collective-permute-start.35 = (bf16[64,2048]{0,1:T(8,128)(2,1)S(1)}, bf16[64,2048]{0,1:T(8,128)(2,1)S(1)}, u32[]{:S(2)}, u32[]{:S(2)}) collective-permute-start(bf16[64,2048]{0,1:T(8,128)(2,1)S(1)} %split.139), channel_id=1, source_target_pairs={{0,8},{4,12},{8,0},{12,4},{1,9},{5,13},{9,1},{13,5},{2,10},{6,14},... | collective-permute-start | bytes 786440 | tf_op jit(solution)/shard_map/ppermute | solution.py:109
  427.4 46.9 %collective-permute-start.31 = (bf16[64,2048]{0,1:T(8,128)(2,1)S(1)}, bf16[64,2048]{0,1:T(8,128)(2,1)S(1)}, u32[]{:S(2)}, u32[]{:S(2)}) collective-permute-start(bf16[64,2048]{0,1:T(8,128)(2,1)S(1)} %split.135), channel_id=1, source_target_pairs={{0,8},{4,12},{8,0},{12,4},{1,9},{5,13},{9,1},{13,5},{2,10},{6,14},... | collective-permute-start | bytes 786440 | tf_op jit(solution)/shard_map/ppermute | solution.py:109
  (58 other events, 1353.7 us)
